TPU v7x, 128 devices: a whole 4x4x4 slice. The times are simulated.
128 devices in a mesh: tile: 16 (over y, x), visit: 8 (over z, core).
Axes of the slice: x: 4, y: 4, z: 4, core: 2. Of those that a mesh axis runs over, the one named last changes fastest.
Arguments:
- pixels: bfloat16 [8, 224, 256, 128], P('visit', 'tile'), may hold values from -6 to 6
- dest_block: int32 [8, 224], P('visit', 'tile'), may hold values from 0 to 255, as said below
- phase_index: int32 [8, 224, 2], P('visit', 'tile'), may hold values from 0 to 15
- basis_row: bfloat16 [9, 31], replicated, may hold values from -1 to 1
- basis_col: bfloat16 [9, 31], replicated, may hold values from -1 to 1
- coefficients: float32 [8, 9], P('visit'), may hold values from -2 to 2
- visit_weight: float32 [8], replicated, may hold values from 0.25 to 4
Outputs:
- coadd: float32 [256, 32768], P('visit', 'tile')
Inputs may be any that keep to these rules, and one draw needn't show every extreme that they name: `dest_block`: within one visit the pieces lie on distinct sky blocks. Of the 14 pieces of one visit in rows s * 14 to (s + 1) * 14 - 1, at most 2 lie on the blocks of one tile, and exactly 2 do for some tile.
All inputs are finite; a program needn't handle non-finite values.
Results may differ from a plain program's by a relative error of at most 0.017.
Values may be sent and summed in bfloat16 or wider, within the bound.
No kernel may reach another device: no remote copies, remote signals or barrier semaphores. Data moves between devices by JAX's collectives and lax.ppermute only.
A program may use at most 128 MiB of HBM per device.

v0:
```python
import jax
import jax.numpy as jnp
import numpy as np
from jax import lax
from jax.experimental import pallas as pl
from jax.experimental.pallas import tpu as pltpu
from jax.sharding import PartitionSpec as P

BLOCK = 128
TAPS = 31
HALF = 15
NBASIS = 9
PHASES = 16
PIECES = 14
H = 256
TILES = 16
STRIP = 16
STRIDE = 164
REACH = 18
COLS = 18 * BLOCK
META = PIECES * STRIDE
SKY = 256
F32 = jnp.float32
BF16 = jnp.bfloat16


def tap_table():
    fraction = np.arange(PHASES)[:, None] / PHASES
    distance = np.arange(-3, 4)[None, :] - fraction
    raw = np.sinc(distance) * np.sinc(distance / 4.0)
    return raw / raw.sum(1, keepdims=True)


def row_bases():
    table = np.zeros((PHASES, H), np.float32)
    taps = tap_table()
    for tap in range(7):
        table[:, (tap - 3) % H] = taps[:, tap]
    return table


def col_bases():
    table = np.zeros((PHASES, 3 * BLOCK), np.float32)
    table[:, :7] = tap_table()[:, ::-1]
    return table


def spread(basis, base, width, step):
    lanes = [(base + step * tap) % width for tap in range(TAPS)]
    placing = np.zeros((TAPS, width), np.float32)
    placing[np.arange(TAPS), lanes] = 1.0
    return jnp.dot(basis.astype(F32), placing, precision=lax.Precision.HIGHEST)


def contribute(phase, dest, coef, vw, row_tab, col_tab, rowb, colb, pix, out, call, rall, xbuf, zbuf):
    visit = lax.axis_index("visit")
    total = vw[0]
    for other in range(1, 8):
        total = total + vw[other]
    share = jnp.full((1, BLOCK), vw[visit], F32) / jnp.full((1, BLOCK), total, F32)

    y_of = lax.broadcasted_iota(jnp.int32, (H, H), 0)
    x_of = lax.broadcasted_iota(jnp.int32, (H, H), 1)
    gap = x_of - y_of
    near = jnp.abs(gap) <= HALF
    lag = lax.broadcasted_iota(jnp.int32, (H, BLOCK), 0) - lax.broadcasted_iota(jnp.int32, (H, BLOCK), 1)
    inside = (lag >= 64 - HALF) & (lag <= 64 + HALF)
    for k in range(NBASIS):
        base = jnp.broadcast_to(rowb[k : k + 1, :], (H, H))
        band = pltpu.roll(base, 0, 1, stride=1, stride_axis=0)
        rall[:, k * H : (k + 1) * H] = jnp.where(near, band, 0.0).astype(BF16)
        line = colb[k : k + 1, :] * (share * coef[0, k])
        band = pltpu.roll(jnp.broadcast_to(line, (H, BLOCK)), 0, 1, stride=1, stride_axis=0)
        call[:, k * BLOCK : (k + 1) * BLOCK] = jnp.where(inside, band, 0.0).astype(BF16)

    close = jnp.abs(gap) <= 3
    xbuf[...] = jnp.zeros_like(xbuf)
    for i in range(PIECES):
        base = jnp.broadcast_to(row_tab[pl.ds(phase[i, 0], 1), :], (H, H))
        row_op = pltpu.roll(base, 0, 1, stride=1, stride_axis=0)
        row_op = jnp.where(close, row_op, 0.0).astype(BF16)
        tall = jnp.dot(row_op, pix[0, i], preferred_element_type=F32).astype(BF16)
        start = STRIDE * i + HALF + 64
        block, offset = divmod(start, BLOCK)
        count = -(-(offset + BLOCK + 6) // BLOCK)
        base = pltpu.roll(jnp.broadcast_to(col_tab[pl.ds(phase[i, 1], 1), :], (8, 3 * BLOCK)), offset, 1)
        base = jnp.broadcast_to(base[:1], (BLOCK, 3 * BLOCK))
        col_op = pltpu.roll(base, 0, 1, stride=1, stride_axis=0)[:, : count * BLOCK].astype(BF16)
        window = jnp.dot(tall, col_op, preferred_element_type=F32).astype(BF16)
        span = slice(block * BLOCK, (block + count) * BLOCK)
        xbuf[:, span] = xbuf[:, span] + window

    rows = lax.broadcasted_iota(jnp.int32, (H, BLOCK), 0) % STRIP
    lanes = lax.broadcasted_iota(jnp.int32, (H, BLOCK), 1)
    mark = jnp.zeros((H, BLOCK), F32)
    for i in range(PIECES):
        mark = jnp.where(rows == i, dest[0, i].astype(F32), mark)
    mark = jnp.where(lanes >= META % BLOCK, mark, 0.0)

    def pair(p, carry):
        for side in range(2):
            at = pl.multiple_of(p * 2 * BLOCK + side * BLOCK, BLOCK)
            part = xbuf[:, pl.ds(at, 2 * BLOCK)]
            z = jnp.dot(part, call[...], preferred_element_type=F32).astype(BF16)
            for k in range(NBASIS):
                zbuf[k * H : (k + 1) * H, side * BLOCK : (side + 1) * BLOCK] = z[:, k * BLOCK : (k + 1) * BLOCK]
        got = jnp.dot(rall[...], zbuf[...], preferred_element_type=F32)
        at = pl.multiple_of(p * 2 * BLOCK, BLOCK)
        out[:, :, pl.ds(at, 2 * BLOCK)] = got.astype(BF16).reshape(TILES, STRIP, 2 * BLOCK)
        return carry

    lax.fori_loop(0, COLS // (2 * BLOCK), pair, 0)
    last = out[:, :, COLS - BLOCK :].astype(F32) + mark.reshape(TILES, STRIP, BLOCK)
    out[:, :, COLS - BLOCK :] = last.astype(BF16)


def place(dest, arr, send, keep, main, left, right):
    core = lax.rem(lax.axis_index("visit"), 2)
    for buf in (main, left, right):
        buf[...] = jnp.zeros_like(buf)
    lane = lax.broadcasted_iota(jnp.int32, (STRIP, BLOCK), 1)
    for i in range(PIECES):
        q, o = divmod(STRIDE * i + REACH, BLOCK)

        def one(s, carry, i=i, q=q, o=o):
            def turned(b):
                block = arr[s, :, b * BLOCK : (b + 1) * BLOCK].astype(F32)
                return pltpu.roll(block, (BLOCK - o) % BLOCK, 1)

            first, second = turned(q), turned(q + 1)
            body = jnp.where(lane < BLOCK - o, first, second)
            low = first
            if o < REACH:
                low = jnp.where(lane < BLOCK - o, turned(q - 1), first)
            low = jnp.where(lane >= BLOCK - REACH, low, 0.0)
            high = second
            if o + REACH > BLOCK:
                high = jnp.where(lane < BLOCK - o, second, turned(q + 2))
            high = jnp.where(lane < REACH, high, 0.0)
            d = dest[s, i]
            main[d + 1] = body.astype(BF16)
            left[d] = low.astype(BF16)
            right[d + 2] = high.astype(BF16)
            return carry

        lax.fori_loop(0, TILES, one, 0, unroll=4)

    step = 8

    def total(start):
        picked = [buf[pl.ds(start + 1, step)].astype(F32) for buf in (main, left, right)]
        return picked[0] + picked[1] + picked[2]

    def fill(j, carry):
        send[pl.ds(j * step, step)] = total((1 - core) * 128 + j * step).astype(BF16)
        keep[pl.ds(j * step, step)] = total(core * 128 + j * step)
        return carry

    lax.fori_loop(0, 128 // step, fill, 0, unroll=2)


def on_device(pixels, dest_block, phase_index, basis_row, basis_col, coefficients, visit_weight):
    smem = pl.BlockSpec(memory_space=pltpu.SMEM)
    vmem = pl.BlockSpec(memory_space=pltpu.VMEM)
    rowb = spread(basis_row, -HALF, H, 1)
    colb = spread(basis_col, -(64 - HALF), BLOCK, -1)
    sent = pl.pallas_call(
        contribute,
        out_shape=jax.ShapeDtypeStruct((TILES, STRIP, COLS), BF16),
        in_specs=[smem] * 4 + [vmem] * 5,
        out_specs=vmem,
        scratch_shapes=[
            pltpu.VMEM((H, NBASIS * BLOCK), BF16),
            pltpu.VMEM((H, NBASIS * H), BF16),
            pltpu.VMEM((H, COLS + BLOCK), BF16),
            pltpu.VMEM((NBASIS * H, 2 * BLOCK), BF16),
        ],
        compiler_params=pltpu.CompilerParams(vmem_limit_bytes=40 * 1024 * 1024),
    )(
        phase_index[0], dest_block, coefficients, visit_weight,
        jnp.asarray(row_bases()), jnp.asarray(col_bases()), rowb, colb, pixels,
    )
    arrived = lax.all_to_all(sent, "tile", split_axis=0, concat_axis=0, tiled=True)
    blocks = arrived[:, :PIECES, META].astype(jnp.int32)
    sends, keeps = pl.pallas_call(
        place,
        out_shape=(
            jax.ShapeDtypeStruct((128, STRIP, BLOCK), BF16),
            jax.ShapeDtypeStruct((128, STRIP, BLOCK), F32),
        ),
        in_specs=[smem, vmem],
        out_specs=(vmem, vmem),
        scratch_shapes=[pltpu.VMEM((SKY + 2, STRIP, BLOCK), BF16)] * 3,
        compiler_params=pltpu.CompilerParams(vmem_limit_bytes=40 * 1024 * 1024),
    )(blocks, arrived)
    other = lax.ppermute(sends, "visit", [(i, i ^ 1) for i in range(8)])
    both = (keeps + other.astype(F32)).astype(BF16).reshape(4, 32, STRIP, BLOCK)
    quarters = lax.all_to_all(
        both, "visit", split_axis=0, concat_axis=0, tiled=True,
        axis_index_groups=[[0, 2, 4, 6], [1, 3, 5, 7]],
    )
    summed = jnp.sum(quarters.astype(F32), 0).astype(BF16).reshape(2, 16, STRIP, BLOCK)
    odd = lax.axis_index("tile") % 2 == 1
    parts = [jnp.where(odd, summed[1 - h], summed[h]) for h in range(2)]

    def route(h):
        return [
            (r * 8 + z * 2 + c, (8 * c + 2 * z + (r + h) % 2) * 8 + r // 2)
            for r in range(16) for z in range(4) for c in range(2)
        ]

    got = [lax.ppermute(parts[h], ("tile", "visit"), route(h)) for h in range(2)]
    upper = jnp.where(odd, got[1], got[0])
    lower = jnp.where(odd, got[0], got[1])
    whole = jnp.concatenate([upper, lower], 1).astype(F32)
    return jnp.transpose(whole, (1, 0, 2)).reshape(32, 16 * BLOCK)


def solution(mesh):
    placed = (
        P("visit", "tile", None, None),
        P("visit", "tile"),
        P("visit", "tile", None),
        P(),
        P(),
        P("visit", None),
        P(),
    )
    return jax.shard_map(
        on_device, mesh=mesh, in_specs=placed, out_specs=P("visit", "tile"), check_vma=False
    )
```

profile of v0, /device:TPU:65, one launch (start us, length us, event | category | flops | bytes accessed | tf_op | source)
XLA Modules:
  0.0 84.8 jit_solution(5359759772898626934)
XLA Ops:
  0.0 0.8 copy.15.phase
  0.8 0.8 convolution_bitcast_fusion.1.colb
  1.6 0.9 %convolution_bitcast_fusion.rowb = f32[9,256]{1,0:T(8,128)S(1)} fusion(f32[31,256]{1,0:T(8,128)} %constant.31.clone, bf16[9,31]{1,0:T(8,128)(2,1)S(1)} %copy-done), kind=kOutput, calls=%fused_computation | convolution fusion | flops 857088 | bytes 41518 | tf_op jit(solution)/shard_map/dot_general | solution.py:52
  2.5 1.2 %copy-done.1 = bf16[1,14,256,128]{3,2,1,0:T(8,128)(2,1)S(1)} copy-done((bf16[1,14,256,128]{3,2,1,0:T(8,128)(2,1)S(1)}, bf16[1,14,256,128]{3,2,1,0:T(8,128)(2,1)}, u32[]{:S(2)}) %copy-start.1) | copy-done | bytes 917528
  3.7 0.7 copy-done.2
  4.5 0.7 copy-done.3
  5.2 0.7 copy-done.4
  5.8 0.7 copy-done.5
  6.5 0.7 copy-done.6
  7.1 14.2 %shard_map.109 = bf16[16,16,2304]{2,1,0:T(8,128)(2,1)S(1)} custom-call(s32[14,2]{1,0:T(8,128)S(1)} %copy.15.phase, s32[1,14]{1,0:T(1,128)S(1)} %copy-done.4, f32[1,9]{1,0:T(1,128)S(1)} %copy-done.5, f32[8]{0:T(128)S(1)} %copy-done.6, f32[16,256]{1,0:T(8,128)S(1)} %copy-done.3, f32[16,384]{1,0:T(8,128)S(1)} %copy-done.2, ...), custom_call_target="tpu_custom_call" | custom-call | tf_op jit(solution)/shard_map/pallas_call | solution.py:167
  21.3 24.0 %all_to_all.10.arr = bf16[16,16,2304]{2,1,0:T(8,128)(2,1)S(1)} all-to-all(bf16[16,16,2304]{2,1,0:T(8,128)(2,1)S(1)} %shard_map.109), channel_id=1, replica_groups=mesh['tile'=16,'visit'=8] {'tile'}, dimensions={0} | all-to-all | bytes 2359296 | tf_op jit(solution)/shard_map/all_to_all | solution.py:183
  45.3 0.4 convert_reduce_fusion.dest
  45.7 6.1 %shard_map.110 = (bf16[128,16,128]{2,1,0:T(8,128)(2,1)S(1)}, f32[128,16,128]{2,1,0:T(8,128)S(1)}) custom-call(s32[16,14]{1,0:T(8,128)S(1)} %convert_reduce_fusion.dest, bf16[16,16,2304]{2,1,0:T(8,128)(2,1)S(1)} %all_to_all.10.arr), custom_call_target="tpu_custom_call" | custom-call | tf_op jit(solution)/shard_map/pallas_call | solution.py:185
  51.8 2.2 %collective-permute-start = (bf16[128,16,128]{2,1,0:T(8,128)(2,1)S(1)}, bf16[128,16,128]{2,1,0:T(8,128)(2,1)S(1)}, u32[]{:S(2)}, u32[]{:S(2)}) collective-permute-start(bf16[128,16,128]{2,1,0:T(8,128)(2,1)S(1)} %get-tuple-element.8), channel_id=1, source_target_pairs={{0,1},{1,0},{2,3},{3,2},{4,5},{5,4},{6,7},{7,6},{8,9},{9,8},{10,11... | collective-permute-start | bytes 1572872 | tf_op jit(solution)/shard_map/ppermute | solution.py:196
  54.0 1.5 %collective-permute-done = bf16[128,16,128]{2,1,0:T(8,128)(2,1)S(1)} collective-permute-done((bf16[128,16,128]{2,1,0:T(8,128)(2,1)S(1)}, bf16[128,16,128]{2,1,0:T(8,128)(2,1)S(1)}, u32[]{:S(2)}, u32[]{:S(2)}) %collective-permute-start) | collective-permute-done | bytes 524320 | tf_op jit(solution)/shard_map/ppermute | solution.py:196
  55.5 0.9 %add_convert_fusion = bf16[128,16,128]{2,1,0:T(8,128)(2,1)} fusion(f32[128,16,128]{2,1,0:T(8,128)S(1)} %get-tuple-element.7, bf16[128,16,128]{2,1,0:T(8,128)(2,1)S(1)} %collective-permute-done), kind=kLoop, calls=%fused_computation.2 | loop fusion | flops 786432 | bytes 2097152 | tf_op jit(solution)/shard_map/convert_element_type | solution.py:197
  56.4 4.4 %all-to-all-start.1 = ((bf16[4,32,16,128]{3,2,1,0:T(8,128)(2,1)}), bf16[4,32,16,128]{3,2,1,0:T(8,128)(2,1)S(1)}, u32[]{:S(2)}, u32[]{:S(2)}) async-start(bf16[4,32,16,128]{3,2,1,0:T(8,128)(2,1)} %bitcast.3), calls=%async_computation.1 | async-start | bytes 1048576 | tf_op jit(solution)/shard_map/all_to_all | solution.py:198
  60.8 6.3 %all-to-all-done.1 = bf16[4,32,16,128]{3,2,1,0:T(8,128)(2,1)S(1)} async-done(((bf16[4,32,16,128]{3,2,1,0:T(8,128)(2,1)}), bf16[4,32,16,128]{3,2,1,0:T(8,128)(2,1)S(1)}, u32[]{:S(2)}, u32[]{:S(2)}) %all-to-all-start.1) | async-done | bytes 524320 | tf_op jit(solution)/shard_map/all_to_all | solution.py:198
  67.1 0.1 reduce_sum.12
  67.2 4.4 %collective-permute-start.1 = (bf16[16,16,128]{2,1,0:T(8,128)(2,1)S(1)}, bf16[16,16,128]{2,1,0:T(8,128)(2,1)S(1)}, u32[]{:S(2)}, u32[]{:S(2)}) collective-permute-start(bf16[16,16,128]{2,1,0:T(8,128)(2,1)S(1)} %get-tuple-element.11), channel_id=1, source_target_pairs={{0,8},{1,72},{2,24},{3,88},{4,40},{5,104},{6,56},{7,120},{8,0},{9,... | collective-permute-start | bytes 196616 | tf_op jit(solution)/shard_map/ppermute | solution.py:212
  71.6 4.9 %collective-permute-start.2 = (bf16[16,16,128]{2,1,0:T(8,128)(2,1)S(1)}, bf16[16,16,128]{2,1,0:T(8,128)(2,1)S(1)}, u32[]{:S(2)}, u32[]{:S(2)}) collective-permute-start(bf16[16,16,128]{2,1,0:T(8,128)(2,1)S(1)} %get-tuple-element.12), channel_id=1, source_target_pairs={{0,0},{1,64},{2,16},{3,80},{4,32},{5,96},{6,48},{7,112},{8,8},{9,7... | collective-permute-start | bytes 196616 | tf_op jit(solution)/shard_map/ppermute | solution.py:212
  76.5 2.4 %collective-permute-done.1 = bf16[16,16,128]{2,1,0:T(8,128)(2,1)S(1)} collective-permute-done((bf16[16,16,128]{2,1,0:T(8,128)(2,1)S(1)}, bf16[16,16,128]{2,1,0:T(8,128)(2,1)S(1)}, u32[]{:S(2)}, u32[]{:S(2)}) %collective-permute-start.1) | collective-permute-done | bytes 65568 | tf_op jit(solution)/shard_map/ppermute | solution.py:212
  78.9 5.2 %collective-permute-done.2 = bf16[16,16,128]{2,1,0:T(8,128)(2,1)S(1)} collective-permute-done((bf16[16,16,128]{2,1,0:T(8,128)(2,1)S(1)}, bf16[16,16,128]{2,1,0:T(8,128)(2,1)S(1)}, u32[]{:S(2)}, u32[]{:S(2)}) %collective-permute-start.2) | collective-permute-done | bytes 65568 | tf_op jit(solution)/shard_map/ppermute | solution.py:212
  84.1 0.7 copy_bitcast_fusion
  (10 shorter events, 0.0 us)
Async XLA Ops:
  0.0 1.6 %copy-start = (bf16[9,31]{1,0:T(8,128)(2,1)S(1)}, bf16[9,31]{1,0:T(8,128)(2,1)}, u32[]{:S(2)}) copy-start(bf16[9,31]{1,0:T(8,128)(2,1)} %param.14) | copy-start | bytes 1678
  2.5 1.2 %copy-start.1 = (bf16[1,14,256,128]{3,2,1,0:T(8,128)(2,1)S(1)}, bf16[1,14,256,128]{3,2,1,0:T(8,128)(2,1)}, u32[]{:S(2)}) copy-start(bf16[1,14,256,128]{3,2,1,0:T(8,128)(2,1)} %pix.1) | copy-start | bytes 2752516
  3.7 0.7 copy-start.2
  4.5 0.7 copy-start.3
  5.2 0.7 copy-start.4
  5.8 0.7 copy-start.5
  6.5 0.7 copy-start.6
  51.8 3.7 %collective-permute-start = (bf16[128,16,128]{2,1,0:T(8,128)(2,1)S(1)}, bf16[128,16,128]{2,1,0:T(8,128)(2,1)S(1)}, u32[]{:S(2)}, u32[]{:S(2)}) collective-permute-start(bf16[128,16,128]{2,1,0:T(8,128)(2,1)S(1)} %get-tuple-element.8), channel_id=1, source_target_pairs={{0,1},{1,0},{2,3},{3,2},{4,5},{5,4},{6,7},{7,6},{8,9},{9,8},{10,11... | collective-permute-start | bytes 1572872 | tf_op jit(solution)/shard_map/ppermute | solution.py:196
  56.4 10.7 %all-to-all-start.1 = ((bf16[4,32,16,128]{3,2,1,0:T(8,128)(2,1)}), bf16[4,32,16,128]{3,2,1,0:T(8,128)(2,1)S(1)}, u32[]{:S(2)}, u32[]{:S(2)}) async-start(bf16[4,32,16,128]{3,2,1,0:T(8,128)(2,1)} %bitcast.3), calls=%async_computation.1 | async-start | bytes 1048576 | tf_op jit(solution)/shard_map/all_to_all | solution.py:198
  67.2 11.6 %collective-permute-start.1 = (bf16[16,16,128]{2,1,0:T(8,128)(2,1)S(1)}, bf16[16,16,128]{2,1,0:T(8,128)(2,1)S(1)}, u32[]{:S(2)}, u32[]{:S(2)}) collective-permute-start(bf16[16,16,128]{2,1,0:T(8,128)(2,1)S(1)} %get-tuple-element.11), channel_id=1, source_target_pairs={{0,8},{1,72},{2,24},{3,88},{4,40},{5,104},{6,56},{7,120},{8,0},{9,... | collective-permute-start | bytes 196616 | tf_op jit(solution)/shard_map/ppermute | solution.py:212
  71.6 12.5 %collective-permute-start.2 = (bf16[16,16,128]{2,1,0:T(8,128)(2,1)S(1)}, bf16[16,16,128]{2,1,0:T(8,128)(2,1)S(1)}, u32[]{:S(2)}, u32[]{:S(2)}) collective-permute-start(bf16[16,16,128]{2,1,0:T(8,128)(2,1)S(1)} %get-tuple-element.12), channel_id=1, source_target_pairs={{0,0},{1,64},{2,16},{3,80},{4,32},{5,96},{6,48},{7,112},{8,8},{9,7... | collective-permute-start | bytes 196616 | tf_op jit(solution)/shard_map/ppermute | solution.py:212
where the time goes:
time: 85.4 us; the launch traced here: 84.8 us
  blocking collectives  24 us (28%)
  Pallas kernels  20.2 us (24%)
  starting transfers between devices  15.8 us (19%)
  waiting for transfers between devices  15.4 us (18%)
  local copies, waits for them, and re-layouts  5.39 us (6%)
  other arithmetic  2.15 us (3%)
  matrix products  1.73 us (2%)
    all_to_all x1, blocking collectives, on_device(): lax.all_to_all(sent, 'tile', split_axis=0, concat_axis=0, tiled=True)  24 us
    pallas_call x1, Pallas kernels, on_device(): pl.pallas_call(contribute, out_shape=jax.ShapeDtypeStruct((TILES, STRIP,...  14.2 us
    ppermute x2, starting transfers between devices, on_device(): lax.ppermute(parts[h], ('tile', 'visit'), route(h))  9.26 us
    ppermute x2, waiting for transfers between devices, on_device(): lax.ppermute(parts[h], ('tile', 'visit'), route(h))  7.6 us
    all_to_all x1, waiting for transfers between devices, on_device(): lax.all_to_all(both, 'visit', split_axis=0, concat_axis=0, tiled=True, ax...  6.31 us
    pallas_call x1, Pallas kernels, on_device(): pl.pallas_call(place, out_shape=(jax.ShapeDtypeStruct((128, STRIP, BLOCK)...  6.07 us
    unnamed x14, local copies, waits for them, and re-layouts  4.61 us
    all_to_all x1, starting transfers between devices, on_device(): lax.all_to_all(both, 'visit', split_axis=0, concat_axis=0, tiled=True, ax...  4.4 us
  transfers between devices with their start and end apart: 4, of which 4 were waited for; matrix products, arithmetic and copies ran while one was open for 0% of the time, Pallas kernels for 0%

commit v1 on v0

--- a/solution.py
+++ b/solution.py
@@ -19,6 +19,7 @@
 REACH = 18
 COLS = 18 * BLOCK
 META = PIECES * STRIDE
+PAIRS = COLS // (2 * BLOCK)
 SKY = 256
 F32 = jnp.float32
 BF16 = jnp.bfloat16
@@ -31,87 +32,116 @@
     return raw / raw.sum(1, keepdims=True)
 
 
-def row_bases():
-    table = np.zeros((PHASES, H), np.float32)
+def bases():
+    table = np.zeros((2 * PHASES, 3 * BLOCK), np.float32)
     taps = tap_table()
     for tap in range(7):
-        table[:, (tap - 3) % H] = taps[:, tap]
+        table[:PHASES, (tap - 3) % H] = taps[:, tap]
+        table[PHASES:, 6 - tap] = taps[:, tap]
     return table
 
 
-def col_bases():
-    table = np.zeros((PHASES, 3 * BLOCK), np.float32)
-    table[:, :7] = tap_table()[:, ::-1]
-    return table
-
-
-def spread(basis, base, width, step):
-    lanes = [(base + step * tap) % width for tap in range(TAPS)]
-    placing = np.zeros((TAPS, width), np.float32)
-    placing[np.arange(TAPS), lanes] = 1.0
-    return jnp.dot(basis.astype(F32), placing, precision=lax.Precision.HIGHEST)
-
-
-def contribute(phase, dest, coef, vw, row_tab, col_tab, rowb, colb, pix, out, call, rall, xbuf, zbuf):
+def contribute(
+    phase_in, dest_in, coef_in, vw_in, tab_in, brow_in, bcol_in, pix_in, out,
+    phase, dest, coef, vw, tab, brow, bcol, pix, call, rall, xbuf, zbuf, sems, pix_sems,
+):
+    small = [
+        pltpu.make_async_copy(source, target, sems.at[n])
+        for n, (source, target) in enumerate(
+            [
+                (brow_in, brow), (bcol_in, bcol), (coef_in, coef), (vw_in, vw),
+                (phase_in, phase), (tab_in, tab), (dest_in, dest),
+            ]
+        )
+    ]
+    for copy in small:
+        copy.start()
+    fetches = [
+        pltpu.make_async_copy(pix_in.at[0, i], pix.at[i], pix_sems.at[i]) for i in range(PIECES)
+    ]
+    for copy in fetches:
+        copy.start()
+
+    y_of = lax.broadcasted_iota(jnp.int32, (H, H), 0)
+    x_of = lax.broadcasted_iota(jnp.int32, (H, H), 1)
+    gap = x_of - y_of
+    near = jnp.abs(gap) <= HALF
+    close = jnp.abs(gap) <= 3
+    lag = lax.broadcasted_iota(jnp.int32, (H, BLOCK), 0) - lax.broadcasted_iota(jnp.int32, (H, BLOCK), 1)
+    inside = (lag >= 64 - HALF) & (lag <= 64 + HALF)
+
+    def placing(base, width, step):
+        tap = lax.broadcasted_iota(jnp.int32, (TAPS, width), 0)
+        lane = lax.broadcasted_iota(jnp.int32, (TAPS, width), 1)
+        at = base + step * tap
+        at = jnp.where(at < 0, at + width, at)
+        return jnp.where(lane == at, 1.0, 0.0).astype(BF16)
+
+    for copy in small:
+        copy.wait()
     visit = lax.axis_index("visit")
     total = vw[0]
     for other in range(1, 8):
         total = total + vw[other]
     share = jnp.full((1, BLOCK), vw[visit], F32) / jnp.full((1, BLOCK), total, F32)
-
-    y_of = lax.broadcasted_iota(jnp.int32, (H, H), 0)
-    x_of = lax.broadcasted_iota(jnp.int32, (H, H), 1)
-    gap = x_of - y_of
-    near = jnp.abs(gap) <= HALF
-    lag = lax.broadcasted_iota(jnp.int32, (H, BLOCK), 0) - lax.broadcasted_iota(jnp.int32, (H, BLOCK), 1)
-    inside = (lag >= 64 - HALF) & (lag <= 64 + HALF)
+    rowb = jnp.dot(brow[...], placing(-HALF, H, 1), preferred_element_type=F32)
+    colb = jnp.dot(bcol[...], placing(HALF - 64, BLOCK, -1), preferred_element_type=F32)
+    for k in range(NBASIS):
+        line = colb[k : k + 1, :] * (share * coef[0, k])
+        band = pltpu.roll(jnp.broadcast_to(line, (H, BLOCK)), 0, 1, stride=1, stride_axis=0)
+        call[:, k * BLOCK : (k + 1) * BLOCK] = jnp.where(inside, band, 0.0).astype(BF16)
     for k in range(NBASIS):
         base = jnp.broadcast_to(rowb[k : k + 1, :], (H, H))
         band = pltpu.roll(base, 0, 1, stride=1, stride_axis=0)
         rall[:, k * H : (k + 1) * H] = jnp.where(near, band, 0.0).astype(BF16)
-        line = colb[k : k + 1, :] * (share * coef[0, k])
-        band = pltpu.roll(jnp.broadcast_to(line, (H, BLOCK)), 0, 1, stride=1, stride_axis=0)
-        call[:, k * BLOCK : (k + 1) * BLOCK] = jnp.where(inside, band, 0.0).astype(BF16)
-
-    close = jnp.abs(gap) <= 3
-    xbuf[...] = jnp.zeros_like(xbuf)
-    for i in range(PIECES):
-        base = jnp.broadcast_to(row_tab[pl.ds(phase[i, 0], 1), :], (H, H))
+
+    for copy in fetches:
+        copy.wait()
+    written = set()
+
+    def warp(i):
+        base = jnp.broadcast_to(tab[pl.ds(phase[0, i], 1), :H], (H, H))
         row_op = pltpu.roll(base, 0, 1, stride=1, stride_axis=0)
         row_op = jnp.where(close, row_op, 0.0).astype(BF16)
-        tall = jnp.dot(row_op, pix[0, i], preferred_element_type=F32).astype(BF16)
-        start = STRIDE * i + HALF + 64
-        block, offset = divmod(start, BLOCK)
+        tall = jnp.dot(row_op, pix[i], preferred_element_type=F32).astype(BF16)
+        block, offset = divmod(STRIDE * i + HALF + 64, BLOCK)
         count = -(-(offset + BLOCK + 6) // BLOCK)
-        base = pltpu.roll(jnp.broadcast_to(col_tab[pl.ds(phase[i, 1], 1), :], (8, 3 * BLOCK)), offset, 1)
-        base = jnp.broadcast_to(base[:1], (BLOCK, 3 * BLOCK))
+        base = jnp.broadcast_to(tab[pl.ds(PHASES + phase[1, i], 1), :], (8, 3 * BLOCK))
+        base = jnp.broadcast_to(pltpu.roll(base, offset, 1)[:1], (BLOCK, 3 * BLOCK))
         col_op = pltpu.roll(base, 0, 1, stride=1, stride_axis=0)[:, : count * BLOCK].astype(BF16)
         window = jnp.dot(tall, col_op, preferred_element_type=F32).astype(BF16)
-        span = slice(block * BLOCK, (block + count) * BLOCK)
-        xbuf[:, span] = xbuf[:, span] + window
-
-    rows = lax.broadcasted_iota(jnp.int32, (H, BLOCK), 0) % STRIP
-    lanes = lax.broadcasted_iota(jnp.int32, (H, BLOCK), 1)
-    mark = jnp.zeros((H, BLOCK), F32)
-    for i in range(PIECES):
-        mark = jnp.where(rows == i, dest[0, i].astype(F32), mark)
-    mark = jnp.where(lanes >= META % BLOCK, mark, 0.0)
-
-    def pair(p, carry):
+        for n in range(count):
+            span = slice((block + n) * BLOCK, (block + n + 1) * BLOCK)
+            part = window[:, n * BLOCK : (n + 1) * BLOCK]
+            xbuf[:, span] = xbuf[:, span] + part if block + n in written else part
+            written.add(block + n)
+
+    def columns(p):
         for side in range(2):
-            at = pl.multiple_of(p * 2 * BLOCK + side * BLOCK, BLOCK)
-            part = xbuf[:, pl.ds(at, 2 * BLOCK)]
-            z = jnp.dot(part, call[...], preferred_element_type=F32).astype(BF16)
+            at = (2 * p + side) * BLOCK
+            z = jnp.dot(xbuf[:, at : at + 2 * BLOCK], call[...], preferred_element_type=F32).astype(BF16)
             for k in range(NBASIS):
-                zbuf[k * H : (k + 1) * H, side * BLOCK : (side + 1) * BLOCK] = z[:, k * BLOCK : (k + 1) * BLOCK]
-        got = jnp.dot(rall[...], zbuf[...], preferred_element_type=F32)
-        at = pl.multiple_of(p * 2 * BLOCK, BLOCK)
-        out[:, :, pl.ds(at, 2 * BLOCK)] = got.astype(BF16).reshape(TILES, STRIP, 2 * BLOCK)
-        return carry
-
-    lax.fori_loop(0, COLS // (2 * BLOCK), pair, 0)
-    last = out[:, :, COLS - BLOCK :].astype(F32) + mark.reshape(TILES, STRIP, BLOCK)
-    out[:, :, COLS - BLOCK :] = last.astype(BF16)
+                zbuf[p % 2, k * H : (k + 1) * H, side * BLOCK : (side + 1) * BLOCK] = z[:, k * BLOCK : (k + 1) * BLOCK]
+
+    def rows(p):
+        got = jnp.dot(rall[...], zbuf[p % 2], preferred_element_type=F32)
+        if p == PAIRS - 1:
+            row = lax.broadcasted_iota(jnp.int32, (H, 2 * BLOCK), 0) % STRIP
+            lane = lax.broadcasted_iota(jnp.int32, (H, 2 * BLOCK), 1)
+            for i in range(PIECES):
+                here = (row == i) & (lane >= META % (2 * BLOCK))
+                got = jnp.where(here, dest[0, i].astype(F32), got)
+        out[:, :, 2 * p * BLOCK : 2 * (p + 1) * BLOCK] = got.astype(BF16).reshape(TILES, STRIP, 2 * BLOCK)
+
+    done = 0
+    for p in range(PAIRS + 1):
+        while done < PIECES and STRIDE * done + HALF + 64 < (2 * p + 3) * BLOCK:
+            warp(done)
+            done += 1
+        if p < PAIRS:
+            columns(p)
+        if p > 0:
+            rows(p - 1)
 
 
 def place(dest, arr, send, keep, main, left, right):
@@ -143,7 +173,7 @@
             right[d + 2] = high.astype(BF16)
             return carry
 
-        lax.fori_loop(0, TILES, one, 0, unroll=4)
+        lax.fori_loop(0, TILES, one, 0, unroll=TILES)
 
     step = 8
 
@@ -162,23 +192,31 @@
 def on_device(pixels, dest_block, phase_index, basis_row, basis_col, coefficients, visit_weight):
     smem = pl.BlockSpec(memory_space=pltpu.SMEM)
     vmem = pl.BlockSpec(memory_space=pltpu.VMEM)
-    rowb = spread(basis_row, -HALF, H, 1)
-    colb = spread(basis_col, -(64 - HALF), BLOCK, -1)
     sent = pl.pallas_call(
         contribute,
         out_shape=jax.ShapeDtypeStruct((TILES, STRIP, COLS), BF16),
-        in_specs=[smem] * 4 + [vmem] * 5,
+        in_specs=[pl.BlockSpec(memory_space=pltpu.HBM)] * 8,
         out_specs=vmem,
         scratch_shapes=[
+            pltpu.SMEM((2, PIECES), jnp.int32),
+            pltpu.SMEM((1, PIECES), jnp.int32),
+            pltpu.SMEM((1, NBASIS), F32),
+            pltpu.SMEM((8,), F32),
+            pltpu.VMEM((2 * PHASES, 3 * BLOCK), F32),
+            pltpu.VMEM((NBASIS, TAPS), BF16),
+            pltpu.VMEM((NBASIS, TAPS), BF16),
+            pltpu.VMEM((PIECES, H, BLOCK), BF16),
             pltpu.VMEM((H, NBASIS * BLOCK), BF16),
             pltpu.VMEM((H, NBASIS * H), BF16),
             pltpu.VMEM((H, COLS + BLOCK), BF16),
-            pltpu.VMEM((NBASIS * H, 2 * BLOCK), BF16),
+            pltpu.VMEM((2, NBASIS * H, 2 * BLOCK), BF16),
+            pltpu.SemaphoreType.DMA((7,)),
+            pltpu.SemaphoreType.DMA((PIECES,)),
         ],
-        compiler_params=pltpu.CompilerParams(vmem_limit_bytes=40 * 1024 * 1024),
+        compiler_params=pltpu.CompilerParams(vmem_limit_bytes=60 * 1024 * 1024),
     )(
-        phase_index[0], dest_block, coefficients, visit_weight,
-        jnp.asarray(row_bases()), jnp.asarray(col_bases()), rowb, colb, pixels,
+        phase_index[0].T, dest_block, coefficients, visit_weight,
+        jnp.asarray(bases()), basis_row, basis_col, pixels,
     )
     arrived = lax.all_to_all(sent, "tile", split_axis=0, concat_axis=0, tiled=True)
     blocks = arrived[:, :PIECES, META].astype(jnp.int32)

time: 85.4 us -> 70.8 us (0.83)
  Pallas kernels: 20.2 us -> 12.8 us
  local copies, waits for them, and re-layouts: 5.39 us -> 0 us
  matrix products: 1.73 us -> 0 us
    unnamed x14 -> x0, local copies, waits for them, and re-layouts: 4.61 us -> none
    pallas_call x1, Pallas kernels: 6.07 us -> 2.08 us  [on_device(): pl.pallas_call(place, out_shape=(jax.ShapeDtypeStruct((128, STRIP, BLOCK)...]
    pallas_call x1, Pallas kernels: 14.2 us -> 10.7 us  [on_device(): pl.pallas_call(contribute, out_shape=jax.ShapeDtypeStruct((TILES, STRIP,...]
    dot_general x2 -> x0, matrix products: 1.73 us -> none  [spread(): return jnp.dot(basis.astype(F32), placing, precision=lax.Precision.HIGHEST)]
where the time goes in v1:
time: 70.8 us; the launch traced here: 70.5 us
  blocking collectives  24.2 us (34%)
  starting transfers between devices  15.8 us (22%)
  waiting for transfers between devices  15.4 us (22%)
  Pallas kernels  12.8 us (18%)
  other arithmetic  2.15 us (3%)
    all_to_all x1, blocking collectives, on_device(): lax.all_to_all(sent, 'tile', split_axis=0, concat_axis=0, tiled=True)  24.2 us
    pallas_call x1, Pallas kernels, on_device(): pl.pallas_call(contribute, out_shape=jax.ShapeDtypeStruct((TILES, STRIP,...  10.7 us
    ppermute x2, starting transfers between devices, on_device(): lax.ppermute(parts[h], ('tile', 'visit'), route(h))  9.26 us
    ppermute x2, waiting for transfers between devices, on_device(): lax.ppermute(parts[h], ('tile', 'visit'), route(h))  7.6 us
    all_to_all x1, waiting for transfers between devices, on_device(): lax.all_to_all(both, 'visit', split_axis=0, concat_axis=0, tiled=True, ax...  6.31 us
    all_to_all x1, starting transfers between devices, on_device(): lax.all_to_all(both, 'visit', split_axis=0, concat_axis=0, tiled=True, ax...  4.4 us
    ppermute x1, starting transfers between devices, on_device(): other = lax.ppermute(sends, 'visit', [(i, i ^ 1) for i in range(8)])  2.17 us
    pallas_call x1, Pallas kernels, on_device(): pl.pallas_call(place, out_shape=(jax.ShapeDtypeStruct((128, STRIP, BLOCK)...  2.08 us
  transfers between devices with their start and end apart: 4, of which 4 were waited for; matrix products, arithmetic and copies ran while one was open for 0% of the time, Pallas kernels for 0%

profile of v1, /device:TPU:65, one launch (start us, length us, event | category | flops | bytes accessed | tf_op | source)
XLA Modules:
  0.0 70.5 jit_solution(14805326853951172222)
XLA Ops:
  0.0 10.7 %shard_map.82 = bf16[16,16,2304]{2,1,0:T(8,128)(2,1)} custom-call(s32[2,14]{1,0:T(2,128)} %bitcast.10, s32[1,14]{1,0:T(1,128)} %dest_in.1, f32[1,9]{1,0:T(1,128)} %coef_in.1, f32[8]{0:T(128)} %vw_in.1, f32[32,384]{1,0:T(8,128)} %constant.25.clone.tab_in, bf16[9,31]{1,0:T(8,128)(2,1)} %brow_in.1, bf16[9,31]{1,0:T(8,128)(2,1)} %bcol_in.1, ...), custom_call_target="tpu_custom_call" | custom-call | tf_op jit(solution)/shard_map/pallas_call | solution.py:195
  10.7 24.2 %all_to_all.10.arr = bf16[16,16,2304]{2,1,0:T(8,128)(2,1)S(1)} all-to-all(bf16[16,16,2304]{2,1,0:T(8,128)(2,1)} %shard_map.82), channel_id=1, replica_groups=mesh['tile'=16,'visit'=8] {'tile'}, dimensions={0} | all-to-all | bytes 2359296 | tf_op jit(solution)/shard_map/all_to_all | solution.py:221
  34.9 0.4 convert_reduce_fusion.dest
  35.3 2.1 %shard_map.83 = (bf16[128,16,128]{2,1,0:T(8,128)(2,1)S(1)}, f32[128,16,128]{2,1,0:T(8,128)S(1)}) custom-call(s32[16,14]{1,0:T(8,128)S(1)} %convert_reduce_fusion.dest, bf16[16,16,2304]{2,1,0:T(8,128)(2,1)S(1)} %all_to_all.10.arr), custom_call_target="tpu_custom_call" | custom-call | tf_op jit(solution)/shard_map/pallas_call | solution.py:223
  37.4 2.2 %collective-permute-start = (bf16[128,16,128]{2,1,0:T(8,128)(2,1)S(1)}, bf16[128,16,128]{2,1,0:T(8,128)(2,1)S(1)}, u32[]{:S(2)}, u32[]{:S(2)}) collective-permute-start(bf16[128,16,128]{2,1,0:T(8,128)(2,1)S(1)} %get-tuple-element.8), channel_id=1, source_target_pairs={{0,1},{1,0},{2,3},{3,2},{4,5},{5,4},{6,7},{7,6},{8,9},{9,8},{10,11... | collective-permute-start | bytes 1572872 | tf_op jit(solution)/shard_map/ppermute | solution.py:234
  39.6 1.5 %collective-permute-done = bf16[128,16,128]{2,1,0:T(8,128)(2,1)S(1)} collective-permute-done((bf16[128,16,128]{2,1,0:T(8,128)(2,1)S(1)}, bf16[128,16,128]{2,1,0:T(8,128)(2,1)S(1)}, u32[]{:S(2)}, u32[]{:S(2)}) %collective-permute-start) | collective-permute-done | bytes 524320 | tf_op jit(solution)/shard_map/ppermute | solution.py:234
  41.1 0.9 %add_convert_fusion = bf16[128,16,128]{2,1,0:T(8,128)(2,1)} fusion(f32[128,16,128]{2,1,0:T(8,128)S(1)} %get-tuple-element.7, bf16[128,16,128]{2,1,0:T(8,128)(2,1)S(1)} %collective-permute-done), kind=kLoop, calls=%fused_computation | loop fusion | flops 786432 | bytes 2097152 | tf_op jit(solution)/shard_map/convert_element_type | solution.py:235
  42.0 4.4 %all-to-all-start.1 = ((bf16[4,32,16,128]{3,2,1,0:T(8,128)(2,1)}), bf16[4,32,16,128]{3,2,1,0:T(8,128)(2,1)S(1)}, u32[]{:S(2)}, u32[]{:S(2)}) async-start(bf16[4,32,16,128]{3,2,1,0:T(8,128)(2,1)} %bitcast.2), calls=%async_computation.1 | async-start | bytes 1048576 | tf_op jit(solution)/shard_map/all_to_all | solution.py:236
  46.4 6.3 %all-to-all-done.1 = bf16[4,32,16,128]{3,2,1,0:T(8,128)(2,1)S(1)} async-done(((bf16[4,32,16,128]{3,2,1,0:T(8,128)(2,1)}), bf16[4,32,16,128]{3,2,1,0:T(8,128)(2,1)S(1)}, u32[]{:S(2)}, u32[]{:S(2)}) %all-to-all-start.1) | async-done | bytes 524320 | tf_op jit(solution)/shard_map/all_to_all | solution.py:236
  52.8 0.1 reduce_sum.12
  52.9 4.4 %collective-permute-start.1 = (bf16[16,16,128]{2,1,0:T(8,128)(2,1)S(1)}, bf16[16,16,128]{2,1,0:T(8,128)(2,1)S(1)}, u32[]{:S(2)}, u32[]{:S(2)}) collective-permute-start(bf16[16,16,128]{2,1,0:T(8,128)(2,1)S(1)} %get-tuple-element.11), channel_id=1, source_target_pairs={{0,8},{1,72},{2,24},{3,88},{4,40},{5,104},{6,56},{7,120},{8,0},{9,... | collective-permute-start | bytes 196616 | tf_op jit(solution)/shard_map/ppermute | solution.py:250
  57.2 4.9 %collective-permute-start.2 = (bf16[16,16,128]{2,1,0:T(8,128)(2,1)S(1)}, bf16[16,16,128]{2,1,0:T(8,128)(2,1)S(1)}, u32[]{:S(2)}, u32[]{:S(2)}) collective-permute-start(bf16[16,16,128]{2,1,0:T(8,128)(2,1)S(1)} %get-tuple-element.12), channel_id=1, source_target_pairs={{0,0},{1,64},{2,16},{3,80},{4,32},{5,96},{6,48},{7,112},{8,8},{9,7... | collective-permute-start | bytes 196616 | tf_op jit(solution)/shard_map/ppermute | solution.py:250
  62.1 2.4 %collective-permute-done.1 = bf16[16,16,128]{2,1,0:T(8,128)(2,1)S(1)} collective-permute-done((bf16[16,16,128]{2,1,0:T(8,128)(2,1)S(1)}, bf16[16,16,128]{2,1,0:T(8,128)(2,1)S(1)}, u32[]{:S(2)}, u32[]{:S(2)}) %collective-permute-start.1) | collective-permute-done | bytes 65568 | tf_op jit(solution)/shard_map/ppermute | solution.py:250
  64.5 5.2 %collective-permute-done.2 = bf16[16,16,128]{2,1,0:T(8,128)(2,1)S(1)} collective-permute-done((bf16[16,16,128]{2,1,0:T(8,128)(2,1)S(1)}, bf16[16,16,128]{2,1,0:T(8,128)(2,1)S(1)}, u32[]{:S(2)}, u32[]{:S(2)}) %collective-permute-start.2) | collective-permute-done | bytes 65568 | tf_op jit(solution)/shard_map/ppermute | solution.py:250
  69.7 0.7 %copy_bitcast_fusion = f32[32,2048]{1,0:T(8,128)} fusion(bf16[16,16,128]{2,1,0:T(8,128)(2,1)S(1)} %get-tuple-element.10, bf16[16,16,128]{2,1,0:T(8,128)(2,1)S(1)} %get-tuple-element.9), kind=kLoop, calls=%fused_computation.1 | loop fusion | flops 262144 | bytes 393216 | tf_op jit(solution)/shard_map/reshape | solution.py:254
  (2 shorter events, 0.0 us)
Async XLA Ops:
  37.4 3.7 %collective-permute-start = (bf16[128,16,128]{2,1,0:T(8,128)(2,1)S(1)}, bf16[128,16,128]{2,1,0:T(8,128)(2,1)S(1)}, u32[]{:S(2)}, u32[]{:S(2)}) collective-permute-start(bf16[128,16,128]{2,1,0:T(8,128)(2,1)S(1)} %get-tuple-element.8), channel_id=1, source_target_pairs={{0,1},{1,0},{2,3},{3,2},{4,5},{5,4},{6,7},{7,6},{8,9},{9,8},{10,11... | collective-permute-start | bytes 1572872 | tf_op jit(solution)/shard_map/ppermute | solution.py:234
  42.0 10.7 %all-to-all-start.1 = ((bf16[4,32,16,128]{3,2,1,0:T(8,128)(2,1)}), bf16[4,32,16,128]{3,2,1,0:T(8,128)(2,1)S(1)}, u32[]{:S(2)}, u32[]{:S(2)}) async-start(bf16[4,32,16,128]{3,2,1,0:T(8,128)(2,1)} %bitcast.2), calls=%async_computation.1 | async-start | bytes 1048576 | tf_op jit(solution)/shard_map/all_to_all | solution.py:236
  52.9 11.6 %collective-permute-start.1 = (bf16[16,16,128]{2,1,0:T(8,128)(2,1)S(1)}, bf16[16,16,128]{2,1,0:T(8,128)(2,1)S(1)}, u32[]{:S(2)}, u32[]{:S(2)}) collective-permute-start(bf16[16,16,128]{2,1,0:T(8,128)(2,1)S(1)} %get-tuple-element.11), channel_id=1, source_target_pairs={{0,8},{1,72},{2,24},{3,88},{4,40},{5,104},{6,56},{7,120},{8,0},{9,... | collective-permute-start | bytes 196616 | tf_op jit(solution)/shard_map/ppermute | solution.py:250
  57.2 12.5 %collective-permute-start.2 = (bf16[16,16,128]{2,1,0:T(8,128)(2,1)S(1)}, bf16[16,16,128]{2,1,0:T(8,128)(2,1)S(1)}, u32[]{:S(2)}, u32[]{:S(2)}) collective-permute-start(bf16[16,16,128]{2,1,0:T(8,128)(2,1)S(1)} %get-tuple-element.12), channel_id=1, source_target_pairs={{0,0},{1,64},{2,16},{3,80},{4,32},{5,96},{6,48},{7,112},{8,8},{9,7... | collective-permute-start | bytes 196616 | tf_op jit(solution)/shard_map/ppermute | solution.py:250

commit v2 on v1

--- a/solution.py
+++ b/solution.py
@@ -20,6 +20,7 @@
 COLS = 18 * BLOCK
 META = PIECES * STRIDE
 PAIRS = COLS // (2 * BLOCK)
+FETCH = 7
 SKY = 256
 F32 = jnp.float32
 BF16 = jnp.bfloat16
@@ -57,7 +58,8 @@
     for copy in small:
         copy.start()
     fetches = [
-        pltpu.make_async_copy(pix_in.at[0, i], pix.at[i], pix_sems.at[i]) for i in range(PIECES)
+        pltpu.make_async_copy(pix_in.at[0, pl.ds(i, FETCH)], pix.at[pl.ds(i, FETCH)], pix_sems.at[i // FETCH])
+        for i in range(0, PIECES, FETCH)
     ]
     for copy in fetches:
         copy.start()
@@ -125,13 +127,18 @@
 
     def rows(p):
         got = jnp.dot(rall[...], zbuf[p % 2], preferred_element_type=F32)
-        if p == PAIRS - 1:
-            row = lax.broadcasted_iota(jnp.int32, (H, 2 * BLOCK), 0) % STRIP
-            lane = lax.broadcasted_iota(jnp.int32, (H, 2 * BLOCK), 1)
-            for i in range(PIECES):
-                here = (row == i) & (lane >= META % (2 * BLOCK))
-                got = jnp.where(here, dest[0, i].astype(F32), got)
-        out[:, :, 2 * p * BLOCK : 2 * (p + 1) * BLOCK] = got.astype(BF16).reshape(TILES, STRIP, 2 * BLOCK)
+        for strip in range(TILES):
+            z, x = divmod(strip, 4)
+            halves = [got[64 * z + 32 * c + 8 * x : 64 * z + 32 * c + 8 * x + 8] for c in range(2)]
+            both = jnp.concatenate(halves, 0)
+            if p == PAIRS - 1:
+                row = lax.broadcasted_iota(jnp.int32, (STRIP, 2 * BLOCK), 0)
+                lane = lax.broadcasted_iota(jnp.int32, (STRIP, 2 * BLOCK), 1)
+                mark = jnp.zeros((STRIP, 2 * BLOCK), F32)
+                for i in range(PIECES):
+                    mark = jnp.where(row == i, dest[0, i].astype(F32), mark)
+                both = jnp.where(lane >= META % (2 * BLOCK), mark, both)
+            out[strip, :, 2 * p * BLOCK : 2 * (p + 1) * BLOCK] = both.astype(BF16)
 
     done = 0
     for p in range(PAIRS + 1):
@@ -144,15 +151,16 @@
             rows(p - 1)
 
 
-def place(dest, arr, send, keep, main, left, right):
-    core = lax.rem(lax.axis_index("visit"), 2)
-    for buf in (main, left, right):
+def place(dest, arr, send, keep, *bufs):
+    main, left, right = bufs[:4], bufs[4:8], bufs[8:]
+    for buf in bufs:
         buf[...] = jnp.zeros_like(buf)
     lane = lax.broadcasted_iota(jnp.int32, (STRIP, BLOCK), 1)
     for i in range(PIECES):
         q, o = divmod(STRIDE * i + REACH, BLOCK)
-
-        def one(s, carry, i=i, q=q, o=o):
+        for s in range(TILES):
+            z = s // 4
+
             def turned(b):
                 block = arr[s, :, b * BLOCK : (b + 1) * BLOCK].astype(F32)
                 return pltpu.roll(block, (BLOCK - o) % BLOCK, 1)
@@ -168,25 +176,38 @@
                 high = jnp.where(lane < BLOCK - o, second, turned(q + 2))
             high = jnp.where(lane < REACH, high, 0.0)
             d = dest[s, i]
-            main[d + 1] = body.astype(BF16)
-            left[d] = low.astype(BF16)
-            right[d + 2] = high.astype(BF16)
-            return carry
-
-        lax.fori_loop(0, TILES, one, 0, unroll=TILES)
-
-    step = 8
-
-    def total(start):
-        picked = [buf[pl.ds(start + 1, step)].astype(F32) for buf in (main, left, right)]
-        return picked[0] + picked[1] + picked[2]
+            main[z][d + 1] = body.astype(BF16)
+            left[z][d] = low.astype(BF16)
+            right[z][d + 2] = high.astype(BF16)
+
+    upper = lax.rem(lax.axis_index("visit"), 2) == 1
 
     def fill(j, carry):
-        send[pl.ds(j * step, step)] = total((1 - core) * 128 + j * step).astype(BF16)
-        keep[pl.ds(j * step, step)] = total(core * 128 + j * step)
+        for u in range(4):
+            pair = j * 4 + u
+            stays, goes = [], []
+            for side in range(2):
+                terms = [buf[2 * pair + side + 1].astype(F32) for buf in bufs]
+                terms = [terms[n] + terms[n + 6] for n in range(6)]
+                terms = [terms[n] + terms[n + 3] for n in range(3)]
+                terms = [terms[0] + terms[1] + terms[2]]
+                stays.append(jnp.where(upper, terms[0][8:], terms[0][:8]))
+                goes.append(jnp.where(upper, terms[0][:8], terms[0][8:]))
+            send[pair] = jnp.concatenate(goes, 0).astype(BF16)
+            keep[pair] = jnp.concatenate(stays, 0)
         return carry
 
-    lax.fori_loop(0, 128 // step, fill, 0, unroll=2)
+    lax.fori_loop(0, SKY // 8, fill, 0)
+
+
+def gather(arr, out):
+    for x in range(4):
+        for u in range(8):
+            terms = [arr[4 * y + x, u].astype(F32) for y in range(4)]
+            total = (terms[0] + terms[1]) + (terms[2] + terms[3])
+            for side in range(2):
+                at = (2 * u + side) * BLOCK
+                out[8 * x : 8 * x + 8, at : at + BLOCK] = total[8 * side : 8 * side + 8]
 
 
 def on_device(pixels, dest_block, phase_index, basis_row, basis_col, coefficients, visit_weight):
@@ -211,14 +232,20 @@
             pltpu.VMEM((H, COLS + BLOCK), BF16),
             pltpu.VMEM((2, NBASIS * H, 2 * BLOCK), BF16),
             pltpu.SemaphoreType.DMA((7,)),
-            pltpu.SemaphoreType.DMA((PIECES,)),
+            pltpu.SemaphoreType.DMA((PIECES // FETCH,)),
         ],
         compiler_params=pltpu.CompilerParams(vmem_limit_bytes=60 * 1024 * 1024),
     )(
         phase_index[0].T, dest_block, coefficients, visit_weight,
         jnp.asarray(bases()), basis_row, basis_col, pixels,
     )
-    arrived = lax.all_to_all(sent, "tile", split_axis=0, concat_axis=0, tiled=True)
+    groups = [
+        [(4 * y + x) * 8 + 2 * z + c for z in range(4) for x in range(4)]
+        for c in range(2) for y in range(4)
+    ]
+    arrived = lax.all_to_all(
+        sent, ("tile", "visit"), split_axis=0, concat_axis=0, tiled=True, axis_index_groups=groups
+    )
     blocks = arrived[:, :PIECES, META].astype(jnp.int32)
     sends, keeps = pl.pallas_call(
         place,
@@ -228,30 +255,18 @@
         ),
         in_specs=[smem, vmem],
         out_specs=(vmem, vmem),
-        scratch_shapes=[pltpu.VMEM((SKY + 2, STRIP, BLOCK), BF16)] * 3,
+        scratch_shapes=[pltpu.VMEM((SKY + 2, STRIP, BLOCK), BF16)] * 12,
         compiler_params=pltpu.CompilerParams(vmem_limit_bytes=40 * 1024 * 1024),
     )(blocks, arrived)
     other = lax.ppermute(sends, "visit", [(i, i ^ 1) for i in range(8)])
-    both = (keeps + other.astype(F32)).astype(BF16).reshape(4, 32, STRIP, BLOCK)
-    quarters = lax.all_to_all(
-        both, "visit", split_axis=0, concat_axis=0, tiled=True,
-        axis_index_groups=[[0, 2, 4, 6], [1, 3, 5, 7]],
-    )
-    summed = jnp.sum(quarters.astype(F32), 0).astype(BF16).reshape(2, 16, STRIP, BLOCK)
-    odd = lax.axis_index("tile") % 2 == 1
-    parts = [jnp.where(odd, summed[1 - h], summed[h]) for h in range(2)]
-
-    def route(h):
-        return [
-            (r * 8 + z * 2 + c, (8 * c + 2 * z + (r + h) % 2) * 8 + r // 2)
-            for r in range(16) for z in range(4) for c in range(2)
-        ]
-
-    got = [lax.ppermute(parts[h], ("tile", "visit"), route(h)) for h in range(2)]
-    upper = jnp.where(odd, got[1], got[0])
-    lower = jnp.where(odd, got[0], got[1])
-    whole = jnp.concatenate([upper, lower], 1).astype(F32)
-    return jnp.transpose(whole, (1, 0, 2)).reshape(32, 16 * BLOCK)
+    both = (keeps + other.astype(F32)).astype(BF16).reshape(TILES, 8, STRIP, BLOCK)
+    parts = lax.all_to_all(both, "tile", split_axis=0, concat_axis=0, tiled=True)
+    return pl.pallas_call(
+        gather,
+        out_shape=jax.ShapeDtypeStruct((32, 16 * BLOCK), F32),
+        in_specs=[vmem],
+        out_specs=vmem,
+    )(parts)
 
 
 def solution(mesh):

time: 70.8 us -> 63.1 us (0.89)
  the two profiles are of different devices: /device:TPU:65 before, /device:TPU:1 now
where the time goes in v2:
time: 63.1 us; the launch traced here: 62.5 us
  blocking collectives  41.4 us (66%)
  Pallas kernels  16.8 us (27%)
  starting transfers between devices  2.17 us (3%)
  waiting for transfers between devices  1.54 us (2%)
    all_to_all x1, blocking collectives, on_device(): lax.all_to_all(sent, ('tile', 'visit'), split_axis=0, concat_axis=0, tile...  25.9 us
    all_to_all x1, blocking collectives, on_device(): lax.all_to_all(both, 'tile', split_axis=0, concat_axis=0, tiled=True)  15.5 us
    pallas_call x1, Pallas kernels, on_device(): pl.pallas_call(contribute, out_shape=jax.ShapeDtypeStruct((TILES, STRIP,...  10.2 us
    pallas_call x1, Pallas kernels, on_device(): pl.pallas_call(place, out_shape=(jax.ShapeDtypeStruct((128, STRIP, BLOCK)...  4.75 us
    ppermute x1, starting transfers between devices, on_device(): other = lax.ppermute(sends, 'visit', [(i, i ^ 1) for i in range(8)])  2.17 us
    pallas_call x1, Pallas kernels, on_device(): pl.pallas_call(gather, out_shape=jax.ShapeDtypeStruct((32, 16 * BLOCK), F...  1.81 us
    ppermute x1, waiting for transfers between devices, on_device(): other = lax.ppermute(sends, 'visit', [(i, i ^ 1) for i in range(8)])  1.54 us
  transfers between devices with their start and end apart: 1, of which 1 were waited for; matrix products, arithmetic and copies ran while one was open for 0% of the time, Pallas kernels for 0%

profile of v2, /device:TPU:1, one launch (start us, length us, event | category | flops | bytes accessed | tf_op | source)
XLA Modules:
  0.0 62.5 jit_solution(10184746307517760701)
XLA Ops:
  0.0 10.2 %shard_map.82 = bf16[16,16,2304]{2,1,0:T(8,128)(2,1)} custom-call(s32[2,14]{1,0:T(2,128)} %bitcast.5, s32[1,14]{1,0:T(1,128)} %dest_in.1, f32[1,9]{1,0:T(1,128)} %coef_in.1, f32[8]{0:T(128)} %vw_in.1, f32[32,384]{1,0:T(8,128)} %constant.2.clone.tab_in, bf16[9,31]{1,0:T(8,128)(2,1)} %brow_in.1, bf16[9,31]{1,0:T(8,128)(2,1)} %bcol_in.1, ...), custom_call_target="tpu_custom_call" | custom-call | tf_op jit(solution)/shard_map/pallas_call | solution.py:216
  10.3 25.9 %all_to_all.10.arr = bf16[16,16,2304]{2,1,0:T(8,128)(2,1)S(1)} all-to-all(bf16[16,16,2304]{2,1,0:T(8,128)(2,1)} %shard_map.82), channel_id=1, replica_groups={{0,8,16,24,2,10,18,26,4,12,20,28,6,14,22,30},{32,40,48,56,34,42,50,58,3..., dimensions={0} | all-to-all | bytes 2359296 | tf_op jit(solution)/shard_map/all_to_all | solution.py:246
  36.1 0.4 convert_reduce_fusion.dest
  36.5 4.8 %shard_map.83 = (bf16[128,16,128]{2,1,0:T(8,128)(2,1)S(1)}, f32[128,16,128]{2,1,0:T(8,128)S(1)}) custom-call(s32[16,14]{1,0:T(8,128)S(1)} %convert_reduce_fusion.dest, bf16[16,16,2304]{2,1,0:T(8,128)(2,1)S(1)} %all_to_all.10.arr), custom_call_target="tpu_custom_call" | custom-call | tf_op jit(solution)/shard_map/pallas_call | solution.py:250
  41.3 2.2 %collective-permute-start = (bf16[128,16,128]{2,1,0:T(8,128)(2,1)S(1)}, bf16[128,16,128]{2,1,0:T(8,128)(2,1)S(1)}, u32[]{:S(2)}, u32[]{:S(2)}) collective-permute-start(bf16[128,16,128]{2,1,0:T(8,128)(2,1)S(1)} %get-tuple-element.8), channel_id=1, source_target_pairs={{0,1},{1,0},{2,3},{3,2},{4,5},{5,4},{6,7},{7,6},{8,9},{9,8},{10,11... | collective-permute-start | bytes 1572872 | tf_op jit(solution)/shard_map/ppermute | solution.py:261
  43.5 1.5 %collective-permute-done = bf16[128,16,128]{2,1,0:T(8,128)(2,1)S(1)} collective-permute-done((bf16[128,16,128]{2,1,0:T(8,128)(2,1)S(1)}, bf16[128,16,128]{2,1,0:T(8,128)(2,1)S(1)}, u32[]{:S(2)}, u32[]{:S(2)}) %collective-permute-start) | collective-permute-done | bytes 524320 | tf_op jit(solution)/shard_map/ppermute | solution.py:261
  45.0 0.1 add_convert_fusion
  45.1 15.5 %all_to_all.11.arr = bf16[16,8,16,128]{3,2,1,0:T(8,128)(2,1)} all-to-all(bf16[16,8,16,128]{3,2,1,0:T(8,128)(2,1)S(1)} %bitcast.4), channel_id=1, replica_groups=mesh['tile'=16,'visit'=8] {'tile'}, dimensions={0} | all-to-all | bytes 1048576 | tf_op jit(solution)/shard_map/all_to_all | solution.py:263
  60.7 1.8 %shard_map.84 = f32[32,2048]{1,0:T(8,128)} custom-call(bf16[16,8,16,128]{3,2,1,0:T(8,128)(2,1)} %all_to_all.11.arr), custom_call_target="tpu_custom_call" | custom-call | tf_op jit(solution)/shard_map/pallas_call | solution.py:264
Async XLA Ops:
  41.3 3.7 %collective-permute-start = (bf16[128,16,128]{2,1,0:T(8,128)(2,1)S(1)}, bf16[128,16,128]{2,1,0:T(8,128)(2,1)S(1)}, u32[]{:S(2)}, u32[]{:S(2)}) collective-permute-start(bf16[128,16,128]{2,1,0:T(8,128)(2,1)S(1)} %get-tuple-element.8), channel_id=1, source_target_pairs={{0,1},{1,0},{2,3},{3,2},{4,5},{5,4},{6,7},{7,6},{8,9},{9,8},{10,11... | collective-permute-start | bytes 1572872 | tf_op jit(solution)/shard_map/ppermute | solution.py:261

commit v3 on v2

--- a/solution.py
+++ b/solution.py
@@ -152,14 +152,14 @@
 
 
 def place(dest, arr, send, keep, *bufs):
-    main, left, right = bufs[:4], bufs[4:8], bufs[8:]
+    main, left, right = bufs
     for buf in bufs:
         buf[...] = jnp.zeros_like(buf)
     lane = lax.broadcasted_iota(jnp.int32, (STRIP, BLOCK), 1)
-    for i in range(PIECES):
-        q, o = divmod(STRIDE * i + REACH, BLOCK)
-        for s in range(TILES):
-            z = s // 4
+    for s in range(TILES):
+        z = s // 4
+        for i in range(PIECES):
+            q, o = divmod(STRIDE * i + REACH, BLOCK)
 
             def turned(b):
                 block = arr[s, :, b * BLOCK : (b + 1) * BLOCK].astype(F32)
@@ -176,9 +176,8 @@
                 high = jnp.where(lane < BLOCK - o, second, turned(q + 2))
             high = jnp.where(lane < REACH, high, 0.0)
             d = dest[s, i]
-            main[z][d + 1] = body.astype(BF16)
-            left[z][d] = low.astype(BF16)
-            right[z][d + 2] = high.astype(BF16)
+            for buf, at, part in ((main, d + 1, body), (left, d, low), (right, d + 2, high)):
+                buf[at] = part if z == 0 else buf[at] + part
 
     upper = lax.rem(lax.axis_index("visit"), 2) == 1
 
@@ -187,17 +186,14 @@
             pair = j * 4 + u
             stays, goes = [], []
             for side in range(2):
-                terms = [buf[2 * pair + side + 1].astype(F32) for buf in bufs]
-                terms = [terms[n] + terms[n + 6] for n in range(6)]
-                terms = [terms[n] + terms[n + 3] for n in range(3)]
-                terms = [terms[0] + terms[1] + terms[2]]
-                stays.append(jnp.where(upper, terms[0][8:], terms[0][:8]))
-                goes.append(jnp.where(upper, terms[0][:8], terms[0][8:]))
+                total = main[2 * pair + side + 1] + left[2 * pair + side + 1] + right[2 * pair + side + 1]
+                stays.append(jnp.where(upper, total[8:], total[:8]))
+                goes.append(jnp.where(upper, total[:8], total[8:]))
             send[pair] = jnp.concatenate(goes, 0).astype(BF16)
             keep[pair] = jnp.concatenate(stays, 0)
         return carry
 
-    lax.fori_loop(0, SKY // 8, fill, 0)
+    lax.fori_loop(0, SKY // 8, fill, 0, unroll=2)
 
 
 def gather(arr, out):
@@ -255,7 +251,7 @@
         ),
         in_specs=[smem, vmem],
         out_specs=(vmem, vmem),
-        scratch_shapes=[pltpu.VMEM((SKY + 2, STRIP, BLOCK), BF16)] * 12,
+        scratch_shapes=[pltpu.VMEM((SKY + 2, STRIP, BLOCK), F32)] * 3,
         compiler_params=pltpu.CompilerParams(vmem_limit_bytes=40 * 1024 * 1024),
     )(blocks, arrived)
     other = lax.ppermute(sends, "visit", [(i, i ^ 1) for i in range(8)])
@@ -266,6 +262,7 @@
         out_shape=jax.ShapeDtypeStruct((32, 16 * BLOCK), F32),
         in_specs=[vmem],
         out_specs=vmem,
+        compiler_params=pltpu.CompilerParams(vmem_limit_bytes=16 * 1024 * 1024),
     )(parts)
 
 

time: 63.1 us -> 59.6 us (0.945)
  Pallas kernels: 16.8 us -> 13.4 us
    pallas_call x1, Pallas kernels: 4.75 us -> 2.44 us  [on_device(): pl.pallas_call(place, out_shape=(jax.ShapeDtypeStruct((128, STRIP, BLOCK)...]
    pallas_call x1, Pallas kernels: 1.81 us -> 0.76 us  [on_device(): pl.pallas_call(gather, out_shape=jax.ShapeDtypeStruct((32, 16 * BLOCK), F...]
where the time goes in v3:
time: 59.6 us; the launch traced here: 59 us
  blocking collectives  41.3 us (69%)
  Pallas kernels  13.4 us (22%)
  starting transfers between devices  2.17 us (4%)
  waiting for transfers between devices  1.54 us (3%)
    all_to_all x1, blocking collectives, on_device(): lax.all_to_all(sent, ('tile', 'visit'), split_axis=0, concat_axis=0, tile...  25.9 us
    all_to_all x1, blocking collectives, on_device(): lax.all_to_all(both, 'tile', split_axis=0, concat_axis=0, tiled=True)  15.4 us
    pallas_call x1, Pallas kernels, on_device(): pl.pallas_call(contribute, out_shape=jax.ShapeDtypeStruct((TILES, STRIP,...  10.2 us
    pallas_call x1, Pallas kernels, on_device(): pl.pallas_call(place, out_shape=(jax.ShapeDtypeStruct((128, STRIP, BLOCK)...  2.44 us
    ppermute x1, starting transfers between devices, on_device(): other = lax.ppermute(sends, 'visit', [(i, i ^ 1) for i in range(8)])  2.17 us
    ppermute x1, waiting for transfers between devices, on_device(): other = lax.ppermute(sends, 'visit', [(i, i ^ 1) for i in range(8)])  1.54 us
  transfers between devices with their start and end apart: 1, of which 1 were waited for; matrix products, arithmetic and copies ran while one was open for 0% of the time, Pallas kernels for 0%

profile of v3, /device:TPU:1, one launch (start us, length us, event | category | flops | bytes accessed | tf_op | source)
XLA Modules:
  0.0 59.0 jit_solution(17502372192169903447)
XLA Ops:
  0.0 10.2 %shard_map.82 = bf16[16,16,2304]{2,1,0:T(8,128)(2,1)} custom-call(s32[2,14]{1,0:T(2,128)} %bitcast.5, s32[1,14]{1,0:T(1,128)} %dest_in.1, f32[1,9]{1,0:T(1,128)} %coef_in.1, f32[8]{0:T(128)} %vw_in.1, f32[32,384]{1,0:T(8,128)} %constant.2.clone.tab_in, bf16[9,31]{1,0:T(8,128)(2,1)} %brow_in.1, bf16[9,31]{1,0:T(8,128)(2,1)} %bcol_in.1, ...), custom_call_target="tpu_custom_call" | custom-call | tf_op jit(solution)/shard_map/pallas_call | solution.py:212
  10.3 25.9 %all_to_all.10.arr = bf16[16,16,2304]{2,1,0:T(8,128)(2,1)S(1)} all-to-all(bf16[16,16,2304]{2,1,0:T(8,128)(2,1)} %shard_map.82), channel_id=1, replica_groups={{0,8,16,24,2,10,18,26,4,12,20,28,6,14,22,30},{32,40,48,56,34,42,50,58,3..., dimensions={0} | all-to-all | bytes 2359296 | tf_op jit(solution)/shard_map/all_to_all | solution.py:242
  36.1 0.4 convert_reduce_fusion.dest
  36.5 2.4 %shard_map.83 = (bf16[128,16,128]{2,1,0:T(8,128)(2,1)S(1)}, f32[128,16,128]{2,1,0:T(8,128)S(1)}) custom-call(s32[16,14]{1,0:T(8,128)S(1)} %convert_reduce_fusion.dest, bf16[16,16,2304]{2,1,0:T(8,128)(2,1)S(1)} %all_to_all.10.arr), custom_call_target="tpu_custom_call" | custom-call | tf_op jit(solution)/shard_map/pallas_call | solution.py:246
  39.0 2.2 %collective-permute-start = (bf16[128,16,128]{2,1,0:T(8,128)(2,1)S(1)}, bf16[128,16,128]{2,1,0:T(8,128)(2,1)S(1)}, u32[]{:S(2)}, u32[]{:S(2)}) collective-permute-start(bf16[128,16,128]{2,1,0:T(8,128)(2,1)S(1)} %get-tuple-element.8), channel_id=1, source_target_pairs={{0,1},{1,0},{2,3},{3,2},{4,5},{5,4},{6,7},{7,6},{8,9},{9,8},{10,11... | collective-permute-start | bytes 1572872 | tf_op jit(solution)/shard_map/ppermute | solution.py:257
  41.2 1.5 %collective-permute-done = bf16[128,16,128]{2,1,0:T(8,128)(2,1)S(1)} collective-permute-done((bf16[128,16,128]{2,1,0:T(8,128)(2,1)S(1)}, bf16[128,16,128]{2,1,0:T(8,128)(2,1)S(1)}, u32[]{:S(2)}, u32[]{:S(2)}) %collective-permute-start) | collective-permute-done | bytes 524320 | tf_op jit(solution)/shard_map/ppermute | solution.py:257
  42.7 0.1 add_convert_fusion
  42.8 15.4 %all_to_all.11.arr = bf16[16,8,16,128]{3,2,1,0:T(8,128)(2,1)S(1)} all-to-all(bf16[16,8,16,128]{3,2,1,0:T(8,128)(2,1)S(1)} %bitcast.4), channel_id=1, replica_groups=mesh['tile'=16,'visit'=8] {'tile'}, dimensions={0} | all-to-all | bytes 1048576 | tf_op jit(solution)/shard_map/all_to_all | solution.py:259
  58.2 0.8 %shard_map.84 = f32[32,2048]{1,0:T(8,128)} custom-call(bf16[16,8,16,128]{3,2,1,0:T(8,128)(2,1)S(1)} %all_to_all.11.arr), custom_call_target="tpu_custom_call" | custom-call | tf_op jit(solution)/shard_map/pallas_call | solution.py:260
Async XLA Ops:
  39.0 3.7 %collective-permute-start = (bf16[128,16,128]{2,1,0:T(8,128)(2,1)S(1)}, bf16[128,16,128]{2,1,0:T(8,128)(2,1)S(1)}, u32[]{:S(2)}, u32[]{:S(2)}) collective-permute-start(bf16[128,16,128]{2,1,0:T(8,128)(2,1)S(1)} %get-tuple-element.8), channel_id=1, source_target_pairs={{0,1},{1,0},{2,3},{3,2},{4,5},{5,4},{6,7},{7,6},{8,9},{9,8},{10,11... | collective-permute-start | bytes 1572872 | tf_op jit(solution)/shard_map/ppermute | solution.py:257

commit v4 on v3

--- a/solution.py
+++ b/solution.py
@@ -21,6 +21,9 @@
 META = PIECES * STRIDE
 PAIRS = COLS // (2 * BLOCK)
 FETCH = 7
+AHEAD = 6
+NEED = 144
+DEPTH = NBASIS * NEED
 SKY = 256
 F32 = jnp.float32
 BF16 = jnp.bfloat16
@@ -37,7 +40,7 @@
     table = np.zeros((2 * PHASES, 3 * BLOCK), np.float32)
     taps = tap_table()
     for tap in range(7):
-        table[:PHASES, (tap - 3) % H] = taps[:, tap]
+        table[:PHASES, (tap - 3) % BLOCK] = taps[:, tap]
         table[PHASES:, 6 - tap] = taps[:, tap]
     return table
 
@@ -64,11 +67,8 @@
     for copy in fetches:
         copy.start()
 
-    y_of = lax.broadcasted_iota(jnp.int32, (H, H), 0)
-    x_of = lax.broadcasted_iota(jnp.int32, (H, H), 1)
-    gap = x_of - y_of
-    near = jnp.abs(gap) <= HALF
-    close = jnp.abs(gap) <= 3
+    edge = lax.broadcasted_iota(jnp.int32, (8, BLOCK), 1)
+    blank = jnp.zeros((BLOCK - 8, BLOCK), F32)
     lag = lax.broadcasted_iota(jnp.int32, (H, BLOCK), 0) - lax.broadcasted_iota(jnp.int32, (H, BLOCK), 1)
     inside = (lag >= 64 - HALF) & (lag <= 64 + HALF)
 
@@ -92,25 +92,34 @@
         line = colb[k : k + 1, :] * (share * coef[0, k])
         band = pltpu.roll(jnp.broadcast_to(line, (H, BLOCK)), 0, 1, stride=1, stride_axis=0)
         call[:, k * BLOCK : (k + 1) * BLOCK] = jnp.where(inside, band, 0.0).astype(BF16)
-    for k in range(NBASIS):
-        base = jnp.broadcast_to(rowb[k : k + 1, :], (H, H))
-        band = pltpu.roll(base, 0, 1, stride=1, stride_axis=0)
-        rall[:, k * H : (k + 1) * H] = jnp.where(near, band, 0.0).astype(BF16)
-
     for copy in fetches:
         copy.wait()
     written = set()
+    talls = {}
+
+    def lift(i):
+        base = jnp.broadcast_to(tab[pl.ds(phase[0, i], 1), :][:, :BLOCK], (BLOCK, BLOCK))
+        ring = pltpu.roll(base, 0, 1, stride=1, stride_axis=0)
+        top, bottom = ring[:8], ring[120:]
+        inner = jnp.concatenate(
+            [jnp.where(edge >= 64, 0.0, top), ring[8:120], jnp.where(edge < 64, 0.0, bottom)], 0
+        ).astype(BF16)
+        beyond = jnp.concatenate([blank, jnp.where(edge < 64, bottom, 0.0)], 0).astype(BF16)
+        before = jnp.concatenate([jnp.where(edge >= 64, top, 0.0), blank], 0).astype(BF16)
+        row_op = jnp.concatenate(
+            [jnp.concatenate([inner, beyond], 1), jnp.concatenate([before, inner], 1)], 0
+        )
+        talls[i] = jnp.dot(row_op, pix[i], preferred_element_type=F32).astype(BF16)
 
     def warp(i):
-        base = jnp.broadcast_to(tab[pl.ds(phase[0, i], 1), :H], (H, H))
-        row_op = pltpu.roll(base, 0, 1, stride=1, stride_axis=0)
-        row_op = jnp.where(close, row_op, 0.0).astype(BF16)
-        tall = jnp.dot(row_op, pix[i], preferred_element_type=F32).astype(BF16)
+        if i + AHEAD < PIECES:
+            lift(i + AHEAD)
+        tall = talls.pop(i)
         block, offset = divmod(STRIDE * i + HALF + 64, BLOCK)
         count = -(-(offset + BLOCK + 6) // BLOCK)
-        base = jnp.broadcast_to(tab[pl.ds(PHASES + phase[1, i], 1), :], (8, 3 * BLOCK))
-        base = jnp.broadcast_to(pltpu.roll(base, offset, 1)[:1], (BLOCK, 3 * BLOCK))
-        col_op = pltpu.roll(base, 0, 1, stride=1, stride_axis=0)[:, : count * BLOCK].astype(BF16)
+        base = jnp.broadcast_to(tab[pl.ds(PHASES + phase[1, i], 1), :][:, : count * BLOCK], (8, count * BLOCK))
+        base = jnp.broadcast_to(pltpu.roll(base, offset, 1)[:1], (BLOCK, count * BLOCK))
+        col_op = pltpu.roll(base, 0, 1, stride=1, stride_axis=0).astype(BF16)
         window = jnp.dot(tall, col_op, preferred_element_type=F32).astype(BF16)
         for n in range(count):
             span = slice((block + n) * BLOCK, (block + n + 1) * BLOCK)
@@ -123,13 +132,22 @@
             at = (2 * p + side) * BLOCK
             z = jnp.dot(xbuf[:, at : at + 2 * BLOCK], call[...], preferred_element_type=F32).astype(BF16)
             for k in range(NBASIS):
-                zbuf[p % 2, k * H : (k + 1) * H, side * BLOCK : (side + 1) * BLOCK] = z[:, k * BLOCK : (k + 1) * BLOCK]
+                zk = z[:, k * BLOCK : (k + 1) * BLOCK]
+                for h in range(2):
+                    at = DEPTH * h + NEED * k
+                    zbuf[p % 2, at : at + NEED, side * BLOCK : (side + 1) * BLOCK] = zk[112 * h : 112 * h + NEED]
 
     def rows(p):
-        got = jnp.dot(rall[...], zbuf[p % 2], preferred_element_type=F32)
+        got = [
+            jnp.dot(
+                rall[h, :, :DEPTH], zbuf[p % 2, DEPTH * h : DEPTH * (h + 1)], preferred_element_type=F32
+            )
+            for h in range(2)
+        ]
         for strip in range(TILES):
             z, x = divmod(strip, 4)
-            halves = [got[64 * z + 32 * c + 8 * x : 64 * z + 32 * c + 8 * x + 8] for c in range(2)]
+            first = 64 * (z % 2) + 8 * x
+            halves = [got[z // 2][first + 32 * c : first + 32 * c + 8] for c in range(2)]
             both = jnp.concatenate(halves, 0)
             if p == PAIRS - 1:
                 row = lax.broadcasted_iota(jnp.int32, (STRIP, 2 * BLOCK), 0)
@@ -140,13 +158,36 @@
                 both = jnp.where(lane >= META % (2 * BLOCK), mark, both)
             out[strip, :, 2 * p * BLOCK : 2 * (p + 1) * BLOCK] = both.astype(BF16)
 
-    done = 0
+    def rbuild():
+        lane = lax.broadcasted_iota(jnp.int32, (BLOCK, H), 1)
+        for h in range(2):
+            for k in range(NBASIS):
+                block, offset = divmod(NEED * k, BLOCK)
+                base = jnp.broadcast_to(rowb[k : k + 1, :], (8, H))
+                base = pltpu.roll(base, offset + STRIP * h, 1)
+                band = pltpu.roll(jnp.broadcast_to(base[:1], (BLOCK, H)), 0, 1, stride=1, stride_axis=0)
+                band = jnp.where((lane >= offset) & (lane < offset + NEED), band, 0.0).astype(BF16)
+                for n in range(2):
+                    span = slice((block + n) * BLOCK, (block + n + 1) * BLOCK)
+                    part = band[:, n * BLOCK : (n + 1) * BLOCK]
+                    rall[h, :, span] = rall[h, :, span] + part if n == 0 and offset else part
+
+    def ready(p):
+        while len(warped) < PIECES and STRIDE * len(warped) + HALF + 64 < (2 * p + 3) * BLOCK:
+            warp(len(warped))
+            warped.append(True)
+
+    warped = []
+    for i in range(AHEAD):
+        lift(i)
+    ready(0)
     for p in range(PAIRS + 1):
-        while done < PIECES and STRIDE * done + HALF + 64 < (2 * p + 3) * BLOCK:
-            warp(done)
-            done += 1
         if p < PAIRS:
             columns(p)
+        if p == 0:
+            rbuild()
+        if p + 1 < PAIRS:
+            ready(p + 1)
         if p > 0:
             rows(p - 1)
 
@@ -224,9 +265,9 @@
             pltpu.VMEM((NBASIS, TAPS), BF16),
             pltpu.VMEM((PIECES, H, BLOCK), BF16),
             pltpu.VMEM((H, NBASIS * BLOCK), BF16),
-            pltpu.VMEM((H, NBASIS * H), BF16),
+            pltpu.VMEM((2, BLOCK, 11 * BLOCK), BF16),
             pltpu.VMEM((H, COLS + BLOCK), BF16),
-            pltpu.VMEM((2, NBASIS * H, 2 * BLOCK), BF16),
+            pltpu.VMEM((2, 2 * DEPTH, 2 * BLOCK), BF16),
             pltpu.SemaphoreType.DMA((7,)),
             pltpu.SemaphoreType.DMA((PIECES // FETCH,)),
         ],

time: 59.6 us -> 58.1 us (0.975)
  Pallas kernels: 13.4 us -> 11.9 us
    pallas_call x1, Pallas kernels: 10.2 us -> 8.7 us  [on_device(): pl.pallas_call(contribute, out_shape=jax.ShapeDtypeStruct((TILES, STRIP,...]
where the time goes in v4:
time: 58.1 us; the launch traced here: 57.5 us
  blocking collectives  41.3 us (71%)
  Pallas kernels  11.9 us (20%)
  starting transfers between devices  2.17 us (4%)
  waiting for transfers between devices  1.54 us (3%)
    all_to_all x1, blocking collectives, on_device(): lax.all_to_all(sent, ('tile', 'visit'), split_axis=0, concat_axis=0, tile...  25.9 us
    all_to_all x1, blocking collectives, on_device(): lax.all_to_all(both, 'tile', split_axis=0, concat_axis=0, tiled=True)  15.4 us
    pallas_call x1, Pallas kernels, on_device(): pl.pallas_call(contribute, out_shape=jax.ShapeDtypeStruct((TILES, STRIP,...  8.7 us
    pallas_call x1, Pallas kernels, on_device(): pl.pallas_call(place, out_shape=(jax.ShapeDtypeStruct((128, STRIP, BLOCK)...  2.44 us
    ppermute x1, starting transfers between devices, on_device(): other = lax.ppermute(sends, 'visit', [(i, i ^ 1) for i in range(8)])  2.17 us
    ppermute x1, waiting for transfers between devices, on_device(): other = lax.ppermute(sends, 'visit', [(i, i ^ 1) for i in range(8)])  1.54 us
  transfers between devices with their start and end apart: 1, of which 1 were waited for; matrix products, arithmetic and copies ran while one was open for 0% of the time, Pallas kernels for 0%

profile of v4, /device:TPU:1, one launch (start us, length us, event | category | flops | bytes accessed | tf_op | source)
XLA Modules:
  0.0 57.5 jit_solution(14930457639501522990)
XLA Ops:
  0.0 8.7 %shard_map.82 = bf16[16,16,2304]{2,1,0:T(8,128)(2,1)} custom-call(s32[2,14]{1,0:T(2,128)} %bitcast.5, s32[1,14]{1,0:T(1,128)} %dest_in.1, f32[1,9]{1,0:T(1,128)} %coef_in.1, f32[8]{0:T(128)} %vw_in.1, f32[32,384]{1,0:T(8,128)} %constant.2.clone.tab_in, bf16[9,31]{1,0:T(8,128)(2,1)} %brow_in.1, bf16[9,31]{1,0:T(8,128)(2,1)} %bcol_in.1, ...), custom_call_target="tpu_custom_call" | custom-call | tf_op jit(solution)/shard_map/pallas_call | solution.py:253
  8.7 25.9 %all_to_all.10.arr = bf16[16,16,2304]{2,1,0:T(8,128)(2,1)S(1)} all-to-all(bf16[16,16,2304]{2,1,0:T(8,128)(2,1)} %shard_map.82), channel_id=1, replica_groups={{0,8,16,24,2,10,18,26,4,12,20,28,6,14,22,30},{32,40,48,56,34,42,50,58,3..., dimensions={0} | all-to-all | bytes 2359296 | tf_op jit(solution)/shard_map/all_to_all | solution.py:283
  34.6 0.4 convert_reduce_fusion.dest
  35.0 2.4 %shard_map.83 = (bf16[128,16,128]{2,1,0:T(8,128)(2,1)S(1)}, f32[128,16,128]{2,1,0:T(8,128)S(1)}) custom-call(s32[16,14]{1,0:T(8,128)S(1)} %convert_reduce_fusion.dest, bf16[16,16,2304]{2,1,0:T(8,128)(2,1)S(1)} %all_to_all.10.arr), custom_call_target="tpu_custom_call" | custom-call | tf_op jit(solution)/shard_map/pallas_call | solution.py:287
  37.4 2.2 %collective-permute-start = (bf16[128,16,128]{2,1,0:T(8,128)(2,1)S(1)}, bf16[128,16,128]{2,1,0:T(8,128)(2,1)S(1)}, u32[]{:S(2)}, u32[]{:S(2)}) collective-permute-start(bf16[128,16,128]{2,1,0:T(8,128)(2,1)S(1)} %get-tuple-element.8), channel_id=1, source_target_pairs={{0,1},{1,0},{2,3},{3,2},{4,5},{5,4},{6,7},{7,6},{8,9},{9,8},{10,11... | collective-permute-start | bytes 1572872 | tf_op jit(solution)/shard_map/ppermute | solution.py:298
  39.6 1.5 %collective-permute-done = bf16[128,16,128]{2,1,0:T(8,128)(2,1)S(1)} collective-permute-done((bf16[128,16,128]{2,1,0:T(8,128)(2,1)S(1)}, bf16[128,16,128]{2,1,0:T(8,128)(2,1)S(1)}, u32[]{:S(2)}, u32[]{:S(2)}) %collective-permute-start) | collective-permute-done | bytes 524320 | tf_op jit(solution)/shard_map/ppermute | solution.py:298
  41.1 0.1 add_convert_fusion
  41.3 15.4 %all_to_all.11.arr = bf16[16,8,16,128]{3,2,1,0:T(8,128)(2,1)S(1)} all-to-all(bf16[16,8,16,128]{3,2,1,0:T(8,128)(2,1)S(1)} %bitcast.4), channel_id=1, replica_groups=mesh['tile'=16,'visit'=8] {'tile'}, dimensions={0} | all-to-all | bytes 1048576 | tf_op jit(solution)/shard_map/all_to_all | solution.py:300
  56.7 0.8 %shard_map.84 = f32[32,2048]{1,0:T(8,128)} custom-call(bf16[16,8,16,128]{3,2,1,0:T(8,128)(2,1)S(1)} %all_to_all.11.arr), custom_call_target="tpu_custom_call" | custom-call | tf_op jit(solution)/shard_map/pallas_call | solution.py:301
Async XLA Ops:
  37.4 3.7 %collective-permute-start = (bf16[128,16,128]{2,1,0:T(8,128)(2,1)S(1)}, bf16[128,16,128]{2,1,0:T(8,128)(2,1)S(1)}, u32[]{:S(2)}, u32[]{:S(2)}) collective-permute-start(bf16[128,16,128]{2,1,0:T(8,128)(2,1)S(1)} %get-tuple-element.8), channel_id=1, source_target_pairs={{0,1},{1,0},{2,3},{3,2},{4,5},{5,4},{6,7},{7,6},{8,9},{9,8},{10,11... | collective-permute-start | bytes 1572872 | tf_op jit(solution)/shard_map/ppermute | solution.py:298

commit v5 on v4

--- a/solution.py
+++ b/solution.py
@@ -1,3 +1,5 @@
+import functools
+
 import jax
 import jax.numpy as jnp
 import numpy as np
@@ -192,11 +194,11 @@
             rows(p - 1)
 
 
-def place(dest, arr, send, keep, *bufs):
-    main, left, right = bufs
-    for buf in bufs:
+def place(goes, dest, arr, out, main, left, right):
+    upper = lax.rem(lax.axis_index("visit"), 2) == (0 if goes else 1)
+    for buf in (main, left, right):
         buf[...] = jnp.zeros_like(buf)
-    lane = lax.broadcasted_iota(jnp.int32, (STRIP, BLOCK), 1)
+    lane = lax.broadcasted_iota(jnp.int32, (8, BLOCK), 1)
     for s in range(TILES):
         z = s // 4
         for i in range(PIECES):
@@ -204,7 +206,7 @@
 
             def turned(b):
                 block = arr[s, :, b * BLOCK : (b + 1) * BLOCK].astype(F32)
-                return pltpu.roll(block, (BLOCK - o) % BLOCK, 1)
+                return pltpu.roll(jnp.where(upper, block[8:], block[:8]), (BLOCK - o) % BLOCK, 1)
 
             first, second = turned(q), turned(q + 1)
             body = jnp.where(lane < BLOCK - o, first, second)
@@ -220,18 +222,14 @@
             for buf, at, part in ((main, d + 1, body), (left, d, low), (right, d + 2, high)):
                 buf[at] = part if z == 0 else buf[at] + part
 
-    upper = lax.rem(lax.axis_index("visit"), 2) == 1
-
     def fill(j, carry):
         for u in range(4):
             pair = j * 4 + u
-            stays, goes = [], []
+            sides = []
             for side in range(2):
-                total = main[2 * pair + side + 1] + left[2 * pair + side + 1] + right[2 * pair + side + 1]
-                stays.append(jnp.where(upper, total[8:], total[:8]))
-                goes.append(jnp.where(upper, total[:8], total[8:]))
-            send[pair] = jnp.concatenate(goes, 0).astype(BF16)
-            keep[pair] = jnp.concatenate(stays, 0)
+                at = 2 * pair + side + 1
+                sides.append(main[at] + left[at] + right[at])
+            out[pair] = jnp.concatenate(sides, 0).astype(out.dtype)
         return carry
 
     lax.fori_loop(0, SKY // 8, fill, 0, unroll=2)
@@ -284,17 +282,19 @@
         sent, ("tile", "visit"), split_axis=0, concat_axis=0, tiled=True, axis_index_groups=groups
     )
     blocks = arrived[:, :PIECES, META].astype(jnp.int32)
-    sends, keeps = pl.pallas_call(
-        place,
-        out_shape=(
-            jax.ShapeDtypeStruct((128, STRIP, BLOCK), BF16),
-            jax.ShapeDtypeStruct((128, STRIP, BLOCK), F32),
-        ),
-        in_specs=[smem, vmem],
-        out_specs=(vmem, vmem),
-        scratch_shapes=[pltpu.VMEM((SKY + 2, STRIP, BLOCK), F32)] * 3,
-        compiler_params=pltpu.CompilerParams(vmem_limit_bytes=40 * 1024 * 1024),
-    )(blocks, arrived)
+
+    def placed(goes):
+        return pl.pallas_call(
+            functools.partial(place, goes),
+            out_shape=jax.ShapeDtypeStruct((SKY // 2, STRIP, BLOCK), BF16 if goes else F32),
+            in_specs=[smem, vmem],
+            out_specs=vmem,
+            scratch_shapes=[pltpu.VMEM((SKY + 2, 8, BLOCK), F32)] * 3,
+            compiler_params=pltpu.CompilerParams(vmem_limit_bytes=40 * 1024 * 1024),
+            cost_estimate=pl.CostEstimate(flops=10**7, bytes_accessed=4 * 10**6, transcendentals=0),
+        )(blocks, arrived)
+
+    sends, keeps = placed(True), placed(False)
     other = lax.ppermute(sends, "visit", [(i, i ^ 1) for i in range(8)])
     both = (keeps + other.astype(F32)).astype(BF16).reshape(TILES, 8, STRIP, BLOCK)
     parts = lax.all_to_all(both, "tile", split_axis=0, concat_axis=0, tiled=True)

time: 58.1 us -> 58 us (level)
  waiting for transfers between devices: 1.54 us -> 0.01 us
  Pallas kernels: 11.9 us -> 13.4 us
    ppermute x1, waiting for transfers between devices: 1.54 us -> 0.01 us  [on_device(): other = lax.ppermute(sends, 'visit', [(i, i ^ 1) for i in range(8)])]
    pallas_call x1 -> x2, Pallas kernels: 2.44 us -> 3.9 us  [placed(): pl.pallas_call(functools.partial(place, goes), out_shape=jax.ShapeDtypeSt...]
  transfers between devices with their start and end apart: 1 -> 1, of which waited for: 1 -> 0; matrix products, arithmetic and copies ran while one was open for 0% -> 0% of each run, Pallas kernels for 0% -> 3%
where the time goes in v5:
time: 58 us; the launch traced here: 57.8 us
  blocking collectives  41.7 us (72%)
  Pallas kernels  13.4 us (23%)
  starting transfers between devices  2.17 us (4%)
    all_to_all x1, blocking collectives, on_device(): lax.all_to_all(sent, ('tile', 'visit'), split_axis=0, concat_axis=0, tile...  25.9 us
    all_to_all x1, blocking collectives, on_device(): lax.all_to_all(both, 'tile', split_axis=0, concat_axis=0, tiled=True)  15.8 us
    pallas_call x1, Pallas kernels, on_device(): pl.pallas_call(contribute, out_shape=jax.ShapeDtypeStruct((TILES, STRIP,...  8.71 us
    pallas_call x2, Pallas kernels, placed(): pl.pallas_call(functools.partial(place, goes), out_shape=jax.ShapeDtypeSt...  3.9 us
    ppermute x1, starting transfers between devices, on_device(): other = lax.ppermute(sends, 'visit', [(i, i ^ 1) for i in range(8)])  2.17 us
  transfers between devices with their start and end apart: 1, of which 0 were waited for; matrix products, arithmetic and copies ran while one was open for 0% of the time, Pallas kernels for 3%

profile of v5, /device:TPU:1, one launch (start us, length us, event | category | flops | bytes accessed | tf_op | source)
XLA Modules:
  0.0 57.8 jit_solution(15272292514070631740)
XLA Ops:
  0.0 8.7 %shard_map.82 = bf16[16,16,2304]{2,1,0:T(8,128)(2,1)} custom-call(s32[2,14]{1,0:T(2,128)} %bitcast.5, s32[1,14]{1,0:T(1,128)} %dest_in.1, f32[1,9]{1,0:T(1,128)} %coef_in.1, f32[8]{0:T(128)} %vw_in.1, f32[32,384]{1,0:T(8,128)} %constant.2.clone.tab_in, bf16[9,31]{1,0:T(8,128)(2,1)} %brow_in.1, bf16[9,31]{1,0:T(8,128)(2,1)} %bcol_in.1, ...), custom_call_target="tpu_custom_call" | custom-call | tf_op jit(solution)/shard_map/pallas_call | solution.py:251
  8.7 25.9 %all_to_all.10.arr = bf16[16,16,2304]{2,1,0:T(8,128)(2,1)S(1)} all-to-all(bf16[16,16,2304]{2,1,0:T(8,128)(2,1)} %shard_map.82), channel_id=1, replica_groups={{0,8,16,24,2,10,18,26,4,12,20,28,6,14,22,30},{32,40,48,56,34,42,50,58,3..., dimensions={0} | all-to-all | bytes 2359296 | tf_op jit(solution)/shard_map/all_to_all | solution.py:281
  34.6 0.4 convert_reduce_fusion.dest
  35.0 2.0 %shard_map.84 = bf16[128,16,128]{2,1,0:T(8,128)(2,1)S(1)} custom-call(s32[16,14]{1,0:T(8,128)S(1)} %convert_reduce_fusion.dest, bf16[16,16,2304]{2,1,0:T(8,128)(2,1)S(1)} %all_to_all.10.arr), custom_call_target="tpu_custom_call" | custom-call | flops 10000000 | bytes 4000000 | tf_op jit(solution)/shard_map/pallas_call | solution.py:287
  37.0 2.2 %collective-permute-start = (bf16[128,16,128]{2,1,0:T(8,128)(2,1)S(1)}, bf16[128,16,128]{2,1,0:T(8,128)(2,1)S(1)}, u32[]{:S(2)}, u32[]{:S(2)}) collective-permute-start(bf16[128,16,128]{2,1,0:T(8,128)(2,1)S(1)} %shard_map.84), channel_id=1, source_target_pairs={{0,1},{1,0},{2,3},{3,2},{4,5},{5,4},{6,7},{7,6},{8,9},{9,8},{10,11... | collective-permute-start | bytes 1572872 | tf_op jit(solution)/shard_map/ppermute | solution.py:298
  39.1 1.9 %shard_map.83 = f32[128,16,128]{2,1,0:T(8,128)S(1)} custom-call(s32[16,14]{1,0:T(8,128)S(1)} %convert_reduce_fusion.dest, bf16[16,16,2304]{2,1,0:T(8,128)(2,1)S(1)} %all_to_all.10.arr), custom_call_target="tpu_custom_call" | custom-call | flops 10000000 | bytes 4000000 | tf_op jit(solution)/shard_map/pallas_call | solution.py:287
  41.1 0.0 collective-permute-done
  41.1 0.1 add_convert_fusion
  41.2 15.8 %all_to_all.11.arr = bf16[16,8,16,128]{3,2,1,0:T(8,128)(2,1)S(1)} all-to-all(bf16[16,8,16,128]{3,2,1,0:T(8,128)(2,1)S(1)} %bitcast.4), channel_id=1, replica_groups=mesh['tile'=16,'visit'=8] {'tile'}, dimensions={0} | all-to-all | bytes 1048576 | tf_op jit(solution)/shard_map/all_to_all | solution.py:300
  57.0 0.8 %shard_map.85 = f32[32,2048]{1,0:T(8,128)} custom-call(bf16[16,8,16,128]{3,2,1,0:T(8,128)(2,1)S(1)} %all_to_all.11.arr), custom_call_target="tpu_custom_call" | custom-call | tf_op jit(solution)/shard_map/pallas_call | solution.py:301
Async XLA Ops:
  37.0 4.1 %collective-permute-start = (bf16[128,16,128]{2,1,0:T(8,128)(2,1)S(1)}, bf16[128,16,128]{2,1,0:T(8,128)(2,1)S(1)}, u32[]{:S(2)}, u32[]{:S(2)}) collective-permute-start(bf16[128,16,128]{2,1,0:T(8,128)(2,1)S(1)} %shard_map.84), channel_id=1, source_target_pairs={{0,1},{1,0},{2,3},{3,2},{4,5},{5,4},{6,7},{7,6},{8,9},{9,8},{10,11... | collective-permute-start | bytes 1572872 | tf_op jit(solution)/shard_map/ppermute | solution.py:298

commit v6 on v5

--- a/solution.py
+++ b/solution.py
@@ -156,7 +156,8 @@
                 lane = lax.broadcasted_iota(jnp.int32, (STRIP, 2 * BLOCK), 1)
                 mark = jnp.zeros((STRIP, 2 * BLOCK), F32)
                 for i in range(PIECES):
-                    mark = jnp.where(row == i, dest[0, i].astype(F32), mark)
+                    here = (row == i // 8) & (lane == META % (2 * BLOCK) + i % 8)
+                    mark = jnp.where(here, dest[0, i].astype(F32), mark)
                 both = jnp.where(lane >= META % (2 * BLOCK), mark, both)
             out[strip, :, 2 * p * BLOCK : 2 * (p + 1) * BLOCK] = both.astype(BF16)
 
@@ -194,10 +195,22 @@
             rows(p - 1)
 
 
-def place(goes, dest, arr, out, main, left, right):
+def place(goes, arr, out, main, left, right, words, dest, sem):
     upper = lax.rem(lax.axis_index("visit"), 2) == (0 if goes else 1)
+    row = lax.broadcasted_iota(jnp.int32, (TILES, BLOCK), 0)
+    lane = lax.broadcasted_iota(jnp.int32, (TILES, BLOCK), 1)
+    low = high = jnp.zeros((TILES, BLOCK), F32)
+    for s in range(TILES):
+        tile = arr[s, :, COLS - BLOCK :].astype(F32)
+        low = jnp.where(row == s, jnp.broadcast_to(tile[0:1], (TILES, BLOCK)), low)
+        high = jnp.where(row == s, jnp.broadcast_to(tile[1:2], (TILES, BLOCK)), high)
+    both = jnp.where(lane >= BLOCK - 8, low, pltpu.roll(high, BLOCK - 8, 1))
+    words[...] = jnp.where(lane >= BLOCK - 16, both, 0.0).astype(jnp.int32)
+    copy = pltpu.make_async_copy(words, dest, sem)
+    copy.start()
     for buf in (main, left, right):
         buf[...] = jnp.zeros_like(buf)
+    copy.wait()
     lane = lax.broadcasted_iota(jnp.int32, (8, BLOCK), 1)
     for s in range(TILES):
         z = s // 4
@@ -218,7 +231,7 @@
             if o + REACH > BLOCK:
                 high = jnp.where(lane < BLOCK - o, second, turned(q + 2))
             high = jnp.where(lane < REACH, high, 0.0)
-            d = dest[s, i]
+            d = dest[s, BLOCK - 8 + i if i < 8 else BLOCK - 24 + i]
             for buf, at, part in ((main, d + 1, body), (left, d, low), (right, d + 2, high)):
                 buf[at] = part if z == 0 else buf[at] + part
 
@@ -246,7 +259,6 @@
 
 
 def on_device(pixels, dest_block, phase_index, basis_row, basis_col, coefficients, visit_weight):
-    smem = pl.BlockSpec(memory_space=pltpu.SMEM)
     vmem = pl.BlockSpec(memory_space=pltpu.VMEM)
     sent = pl.pallas_call(
         contribute,
@@ -281,18 +293,22 @@
     arrived = lax.all_to_all(
         sent, ("tile", "visit"), split_axis=0, concat_axis=0, tiled=True, axis_index_groups=groups
     )
-    blocks = arrived[:, :PIECES, META].astype(jnp.int32)
 
     def placed(goes):
         return pl.pallas_call(
             functools.partial(place, goes),
             out_shape=jax.ShapeDtypeStruct((SKY // 2, STRIP, BLOCK), BF16 if goes else F32),
-            in_specs=[smem, vmem],
+            in_specs=[vmem],
             out_specs=vmem,
-            scratch_shapes=[pltpu.VMEM((SKY + 2, 8, BLOCK), F32)] * 3,
+            scratch_shapes=[pltpu.VMEM((SKY + 2, 8, BLOCK), F32)] * 3
+            + [
+                pltpu.VMEM((TILES, BLOCK), jnp.int32),
+                pltpu.SMEM((TILES, BLOCK), jnp.int32),
+                pltpu.SemaphoreType.DMA,
+            ],
             compiler_params=pltpu.CompilerParams(vmem_limit_bytes=40 * 1024 * 1024),
             cost_estimate=pl.CostEstimate(flops=10**7, bytes_accessed=4 * 10**6, transcendentals=0),
-        )(blocks, arrived)
+        )(arrived)
 
     sends, keeps = placed(True), placed(False)
     other = lax.ppermute(sends, "visit", [(i, i ^ 1) for i in range(8)])

time: 58 us -> 57.8 us (level)
  transfers between devices with their start and end apart: 1 -> 1, of which waited for: 0 -> 0; matrix products, arithmetic and copies ran while one was open for 0% -> 0% of each run, Pallas kernels for 3% -> 4%
where the time goes in v6:
time: 57.8 us; the launch traced here: 57.6 us
  blocking collectives  41.7 us (72%)
  Pallas kernels  13.6 us (24%)
  starting transfers between devices  2.17 us (4%)
    all_to_all x1, blocking collectives, on_device(): lax.all_to_all(sent, ('tile', 'visit'), split_axis=0, concat_axis=0, tile...  25.9 us
    all_to_all x1, blocking collectives, on_device(): lax.all_to_all(both, 'tile', split_axis=0, concat_axis=0, tiled=True)  15.8 us
    pallas_call x1, Pallas kernels, on_device(): pl.pallas_call(contribute, out_shape=jax.ShapeDtypeStruct((TILES, STRIP,...  8.71 us
    pallas_call x2, Pallas kernels, placed(): pl.pallas_call(functools.partial(place, goes), out_shape=jax.ShapeDtypeSt...  4.14 us
    ppermute x1, starting transfers between devices, on_device(): other = lax.ppermute(sends, 'visit', [(i, i ^ 1) for i in range(8)])  2.17 us
  transfers between devices with their start and end apart: 1, of which 0 were waited for; matrix products, arithmetic and copies ran while one was open for 0% of the time, Pallas kernels for 4%

profile of v6, /device:TPU:1, one launch (start us, length us, event | category | flops | bytes accessed | tf_op | source)
XLA Modules:
  0.0 57.6 jit_solution(9862753445469238043)
XLA Ops:
  0.0 8.7 %shard_map.82 = bf16[16,16,2304]{2,1,0:T(8,128)(2,1)} custom-call(s32[2,14]{1,0:T(2,128)} %bitcast.5, s32[1,14]{1,0:T(1,128)} %dest_in.1, f32[1,9]{1,0:T(1,128)} %coef_in.1, f32[8]{0:T(128)} %vw_in.1, f32[32,384]{1,0:T(8,128)} %constant.2.clone.tab_in, bf16[9,31]{1,0:T(8,128)(2,1)} %brow_in.1, bf16[9,31]{1,0:T(8,128)(2,1)} %bcol_in.1, ...), custom_call_target="tpu_custom_call" | custom-call | tf_op jit(solution)/shard_map/pallas_call | solution.py:263
  8.7 25.9 %all_to_all.10.arr = bf16[16,16,2304]{2,1,0:T(8,128)(2,1)S(1)} all-to-all(bf16[16,16,2304]{2,1,0:T(8,128)(2,1)} %shard_map.82), channel_id=1, replica_groups={{0,8,16,24,2,10,18,26,4,12,20,28,6,14,22,30},{32,40,48,56,34,42,50,58,3..., dimensions={0} | all-to-all | bytes 2359296 | tf_op jit(solution)/shard_map/all_to_all | solution.py:293
  34.6 2.1 %shard_map.84 = bf16[128,16,128]{2,1,0:T(8,128)(2,1)S(1)} custom-call(bf16[16,16,2304]{2,1,0:T(8,128)(2,1)S(1)} %all_to_all.10.arr), custom_call_target="tpu_custom_call" | custom-call | flops 10000000 | bytes 4000000 | tf_op jit(solution)/shard_map/pallas_call | solution.py:298
  36.7 2.2 %collective-permute-start = (bf16[128,16,128]{2,1,0:T(8,128)(2,1)S(1)}, bf16[128,16,128]{2,1,0:T(8,128)(2,1)S(1)}, u32[]{:S(2)}, u32[]{:S(2)}) collective-permute-start(bf16[128,16,128]{2,1,0:T(8,128)(2,1)S(1)} %shard_map.84), channel_id=1, source_target_pairs={{0,1},{1,0},{2,3},{3,2},{4,5},{5,4},{6,7},{7,6},{8,9},{9,8},{10,11... | collective-permute-start | bytes 1572872 | tf_op jit(solution)/shard_map/ppermute | solution.py:314
  38.8 2.1 %shard_map.83 = f32[128,16,128]{2,1,0:T(8,128)S(1)} custom-call(bf16[16,16,2304]{2,1,0:T(8,128)(2,1)S(1)} %all_to_all.10.arr), custom_call_target="tpu_custom_call" | custom-call | flops 10000000 | bytes 4000000 | tf_op jit(solution)/shard_map/pallas_call | solution.py:298
  40.9 0.0 collective-permute-done
  40.9 0.1 add_convert_fusion
  41.0 15.8 %all_to_all.11.arr = bf16[16,8,16,128]{3,2,1,0:T(8,128)(2,1)S(1)} all-to-all(bf16[16,8,16,128]{3,2,1,0:T(8,128)(2,1)S(1)} %bitcast.4), channel_id=1, replica_groups=mesh['tile'=16,'visit'=8] {'tile'}, dimensions={0} | all-to-all | bytes 1048576 | tf_op jit(solution)/shard_map/all_to_all | solution.py:316
  56.8 0.8 %shard_map.85 = f32[32,2048]{1,0:T(8,128)} custom-call(bf16[16,8,16,128]{3,2,1,0:T(8,128)(2,1)S(1)} %all_to_all.11.arr), custom_call_target="tpu_custom_call" | custom-call | tf_op jit(solution)/shard_map/pallas_call | solution.py:317
Async XLA Ops:
  36.7 4.2 %collective-permute-start = (bf16[128,16,128]{2,1,0:T(8,128)(2,1)S(1)}, bf16[128,16,128]{2,1,0:T(8,128)(2,1)S(1)}, u32[]{:S(2)}, u32[]{:S(2)}) collective-permute-start(bf16[128,16,128]{2,1,0:T(8,128)(2,1)S(1)} %shard_map.84), channel_id=1, source_target_pairs={{0,1},{1,0},{2,3},{3,2},{4,5},{5,4},{6,7},{7,6},{8,9},{9,8},{10,11... | collective-permute-start | bytes 1572872 | tf_op jit(solution)/shard_map/ppermute | solution.py:314

commit v7 on v6

--- a/solution.py
+++ b/solution.py
@@ -242,7 +242,7 @@
             for side in range(2):
                 at = 2 * pair + side + 1
                 sides.append(main[at] + left[at] + right[at])
-            out[pair] = jnp.concatenate(sides, 0).astype(out.dtype)
+            out[8 * (TILES - 1 - j // 2) + j % 2 * 4 + u] = jnp.concatenate(sides, 0).astype(out.dtype)
         return carry
 
     lax.fori_loop(0, SKY // 8, fill, 0, unroll=2)
@@ -251,7 +251,7 @@
 def gather(arr, out):
     for x in range(4):
         for u in range(8):
-            terms = [arr[4 * y + x, u].astype(F32) for y in range(4)]
+            terms = [arr[TILES - 1 - 4 * y - x, u].astype(F32) for y in range(4)]
             total = (terms[0] + terms[1]) + (terms[2] + terms[3])
             for side in range(2):
                 at = (2 * u + side) * BLOCK
@@ -313,7 +313,10 @@
     sends, keeps = placed(True), placed(False)
     other = lax.ppermute(sends, "visit", [(i, i ^ 1) for i in range(8)])
     both = (keeps + other.astype(F32)).astype(BF16).reshape(TILES, 8, STRIP, BLOCK)
-    parts = lax.all_to_all(both, "tile", split_axis=0, concat_axis=0, tiled=True)
+    backward = [[8 * t + visit for t in reversed(range(TILES))] for visit in range(8)]
+    parts = lax.all_to_all(
+        both, ("tile", "visit"), split_axis=0, concat_axis=0, tiled=True, axis_index_groups=backward
+    )
     return pl.pallas_call(
         gather,
         out_shape=jax.ShapeDtypeStruct((32, 16 * BLOCK), F32),

time: 57.8 us -> 56.6 us (0.979)
  blocking collectives: 41.7 us -> 40.3 us
    all_to_all x1, blocking collectives: 15.8 us -> 14.5 us  [on_device(): lax.all_to_all(both, ('tile', 'visit'), split_axis=0, concat_axis=0, tile...]
where the time goes in v7:
time: 56.6 us; the launch traced here: 56.4 us
  blocking collectives  40.3 us (71%)
  Pallas kernels  13.7 us (24%)
  starting transfers between devices  2.17 us (4%)
    all_to_all x1, blocking collectives, on_device(): lax.all_to_all(sent, ('tile', 'visit'), split_axis=0, concat_axis=0, tile...  25.9 us
    all_to_all x1, blocking collectives, on_device(): lax.all_to_all(both, ('tile', 'visit'), split_axis=0, concat_axis=0, tile...  14.5 us
    pallas_call x1, Pallas kernels, on_device(): pl.pallas_call(contribute, out_shape=jax.ShapeDtypeStruct((TILES, STRIP,...  8.71 us
    pallas_call x2, Pallas kernels, placed(): pl.pallas_call(functools.partial(place, goes), out_shape=jax.ShapeDtypeSt...  4.25 us
    ppermute x1, starting transfers between devices, on_device(): other = lax.ppermute(sends, 'visit', [(i, i ^ 1) for i in range(8)])  2.17 us
  transfers between devices with their start and end apart: 1, of which 0 were waited for; matrix products, arithmetic and copies ran while one was open for 0% of the time, Pallas kernels for 4%

profile of v7, /device:TPU:1, one launch (start us, length us, event | category | flops | bytes accessed | tf_op | source)
XLA Modules:
  0.0 56.4 jit_solution(3514145569303459566)
XLA Ops:
  0.0 8.7 %shard_map.82 = bf16[16,16,2304]{2,1,0:T(8,128)(2,1)} custom-call(s32[2,14]{1,0:T(2,128)} %bitcast.5, s32[1,14]{1,0:T(1,128)} %dest_in.1, f32[1,9]{1,0:T(1,128)} %coef_in.1, f32[8]{0:T(128)} %vw_in.1, f32[32,384]{1,0:T(8,128)} %constant.2.clone.tab_in, bf16[9,31]{1,0:T(8,128)(2,1)} %brow_in.1, bf16[9,31]{1,0:T(8,128)(2,1)} %bcol_in.1, ...), custom_call_target="tpu_custom_call" | custom-call | tf_op jit(solution)/shard_map/pallas_call | solution.py:263
  8.7 25.9 %all_to_all.10.arr = bf16[16,16,2304]{2,1,0:T(8,128)(2,1)S(1)} all-to-all(bf16[16,16,2304]{2,1,0:T(8,128)(2,1)} %shard_map.82), channel_id=1, replica_groups={{0,8,16,24,2,10,18,26,4,12,20,28,6,14,22,30},{32,40,48,56,34,42,50,58,3..., dimensions={0} | all-to-all | bytes 2359296 | tf_op jit(solution)/shard_map/all_to_all | solution.py:293
  34.6 2.1 %shard_map.84 = bf16[128,16,128]{2,1,0:T(8,128)(2,1)S(1)} custom-call(bf16[16,16,2304]{2,1,0:T(8,128)(2,1)S(1)} %all_to_all.10.arr), custom_call_target="tpu_custom_call" | custom-call | flops 10000000 | bytes 4000000 | tf_op jit(solution)/shard_map/pallas_call | solution.py:298
  36.7 2.2 %collective-permute-start = (bf16[128,16,128]{2,1,0:T(8,128)(2,1)S(1)}, bf16[128,16,128]{2,1,0:T(8,128)(2,1)S(1)}, u32[]{:S(2)}, u32[]{:S(2)}) collective-permute-start(bf16[128,16,128]{2,1,0:T(8,128)(2,1)S(1)} %shard_map.84), channel_id=1, source_target_pairs={{0,1},{1,0},{2,3},{3,2},{4,5},{5,4},{6,7},{7,6},{8,9},{9,8},{10,11... | collective-permute-start | bytes 1572872 | tf_op jit(solution)/shard_map/ppermute | solution.py:314
  38.9 2.1 %shard_map.83 = f32[128,16,128]{2,1,0:T(8,128)S(1)} custom-call(bf16[16,16,2304]{2,1,0:T(8,128)(2,1)S(1)} %all_to_all.10.arr), custom_call_target="tpu_custom_call" | custom-call | flops 10000000 | bytes 4000000 | tf_op jit(solution)/shard_map/pallas_call | solution.py:298
  41.0 0.0 collective-permute-done
  41.0 0.1 add_convert_fusion
  41.1 14.5 %all_to_all.11.arr = bf16[16,8,16,128]{3,2,1,0:T(8,128)(2,1)S(1)} all-to-all(bf16[16,8,16,128]{3,2,1,0:T(8,128)(2,1)S(1)} %bitcast.4), channel_id=1, replica_groups={{120,112,104,96,88,80,72,64,56,48,40,32,24,16,8,0},{121,113,105,97,89,8..., dimensions={0} | all-to-all | bytes 1048576 | tf_op jit(solution)/shard_map/all_to_all | solution.py:317
  55.6 0.8 %shard_map.85 = f32[32,2048]{1,0:T(8,128)} custom-call(bf16[16,8,16,128]{3,2,1,0:T(8,128)(2,1)S(1)} %all_to_all.11.arr), custom_call_target="tpu_custom_call" | custom-call | tf_op jit(solution)/shard_map/pallas_call | solution.py:320
Async XLA Ops:
  36.7 4.3 %collective-permute-start = (bf16[128,16,128]{2,1,0:T(8,128)(2,1)S(1)}, bf16[128,16,128]{2,1,0:T(8,128)(2,1)S(1)}, u32[]{:S(2)}, u32[]{:S(2)}) collective-permute-start(bf16[128,16,128]{2,1,0:T(8,128)(2,1)S(1)} %shard_map.84), channel_id=1, source_target_pairs={{0,1},{1,0},{2,3},{3,2},{4,5},{5,4},{6,7},{7,6},{8,9},{9,8},{10,11... | collective-permute-start | bytes 1572872 | tf_op jit(solution)/shard_map/ppermute | solution.py:314

commit v8 on v7

--- a/solution.py
+++ b/solution.py
@@ -159,7 +159,7 @@
                     here = (row == i // 8) & (lane == META % (2 * BLOCK) + i % 8)
                     mark = jnp.where(here, dest[0, i].astype(F32), mark)
                 both = jnp.where(lane >= META % (2 * BLOCK), mark, both)
-            out[strip, :, 2 * p * BLOCK : 2 * (p + 1) * BLOCK] = both.astype(BF16)
+            out[TILES - 1 - strip, :, 2 * p * BLOCK : 2 * (p + 1) * BLOCK] = both.astype(BF16)
 
     def rbuild():
         lane = lax.broadcasted_iota(jnp.int32, (BLOCK, H), 1)
@@ -287,7 +287,7 @@
         jnp.asarray(bases()), basis_row, basis_col, pixels,
     )
     groups = [
-        [(4 * y + x) * 8 + 2 * z + c for z in range(4) for x in range(4)]
+        [(4 * y + x) * 8 + 2 * z + c for z in reversed(range(4)) for x in reversed(range(4))]
         for c in range(2) for y in range(4)
     ]
     arrived = lax.all_to_all(

time: 56.6 us -> 55.3 us (0.977)
  blocking collectives: 40.3 us -> 39.3 us
    all_to_all x1, blocking collectives: 25.9 us -> 24.5 us  [on_device(): lax.all_to_all(sent, ('tile', 'visit'), split_axis=0, concat_axis=0, tile...]
where the time goes in v8:
time: 55.3 us; the launch traced here: 55.1 us
  blocking collectives  39.3 us (71%)
  Pallas kernels  13.7 us (25%)
  starting transfers between devices  1.9 us (3%)
    all_to_all x1, blocking collectives, on_device(): lax.all_to_all(sent, ('tile', 'visit'), split_axis=0, concat_axis=0, tile...  24.5 us
    all_to_all x1, blocking collectives, on_device(): lax.all_to_all(both, ('tile', 'visit'), split_axis=0, concat_axis=0, tile...  14.7 us
    pallas_call x1, Pallas kernels, on_device(): pl.pallas_call(contribute, out_shape=jax.ShapeDtypeStruct((TILES, STRIP,...  8.71 us
    pallas_call x2, Pallas kernels, placed(): pl.pallas_call(functools.partial(place, goes), out_shape=jax.ShapeDtypeSt...  4.25 us
    ppermute x1, starting transfers between devices, on_device(): other = lax.ppermute(sends, 'visit', [(i, i ^ 1) for i in range(8)])  1.9 us
  transfers between devices with their start and end apart: 1, of which 0 were waited for; matrix products, arithmetic and copies ran while one was open for 0% of the time, Pallas kernels for 4%

profile of v8, /device:TPU:1, one launch (start us, length us, event | category | flops | bytes accessed | tf_op | source)
XLA Modules:
  0.0 55.1 jit_solution(17747241963466730454)
XLA Ops:
  0.0 8.7 %shard_map.82 = bf16[16,16,2304]{2,1,0:T(8,128)(2,1)} custom-call(s32[2,14]{1,0:T(2,128)} %bitcast.5, s32[1,14]{1,0:T(1,128)} %dest_in.1, f32[1,9]{1,0:T(1,128)} %coef_in.1, f32[8]{0:T(128)} %vw_in.1, f32[32,384]{1,0:T(8,128)} %constant.2.clone.tab_in, bf16[9,31]{1,0:T(8,128)(2,1)} %brow_in.1, bf16[9,31]{1,0:T(8,128)(2,1)} %bcol_in.1, ...), custom_call_target="tpu_custom_call" | custom-call | tf_op jit(solution)/shard_map/pallas_call | solution.py:263
  8.7 24.5 %all_to_all.10.arr = bf16[16,16,2304]{2,1,0:T(8,128)(2,1)S(1)} all-to-all(bf16[16,16,2304]{2,1,0:T(8,128)(2,1)} %shard_map.82), channel_id=1, replica_groups={{30,22,14,6,28,20,12,4,26,18,10,2,24,16,8,0},{62,54,46,38,60,52,44,36,5..., dimensions={0} | all-to-all | bytes 2359296 | tf_op jit(solution)/shard_map/all_to_all | solution.py:293
  33.3 2.1 %shard_map.84 = bf16[128,16,128]{2,1,0:T(8,128)(2,1)S(1)} custom-call(bf16[16,16,2304]{2,1,0:T(8,128)(2,1)S(1)} %all_to_all.10.arr), custom_call_target="tpu_custom_call" | custom-call | flops 10000000 | bytes 4000000 | tf_op jit(solution)/shard_map/pallas_call | solution.py:298
  35.4 1.9 %collective-permute-start = (bf16[128,16,128]{2,1,0:T(8,128)(2,1)S(1)}, bf16[128,16,128]{2,1,0:T(8,128)(2,1)S(1)}, u32[]{:S(2)}, u32[]{:S(2)}) collective-permute-start(bf16[128,16,128]{2,1,0:T(8,128)(2,1)S(1)} %shard_map.84), channel_id=1, source_target_pairs={{0,1},{1,0},{2,3},{3,2},{4,5},{5,4},{6,7},{7,6},{8,9},{9,8},{10,11... | collective-permute-start | bytes 1572872 | tf_op jit(solution)/shard_map/ppermute | solution.py:314
  37.3 2.1 %shard_map.83 = f32[128,16,128]{2,1,0:T(8,128)S(1)} custom-call(bf16[16,16,2304]{2,1,0:T(8,128)(2,1)S(1)} %all_to_all.10.arr), custom_call_target="tpu_custom_call" | custom-call | flops 10000000 | bytes 4000000 | tf_op jit(solution)/shard_map/pallas_call | solution.py:298
  39.4 0.0 collective-permute-done
  39.4 0.1 add_convert_fusion
  39.6 14.7 %all_to_all.11.arr = bf16[16,8,16,128]{3,2,1,0:T(8,128)(2,1)S(1)} all-to-all(bf16[16,8,16,128]{3,2,1,0:T(8,128)(2,1)S(1)} %bitcast.4), channel_id=1, replica_groups={{120,112,104,96,88,80,72,64,56,48,40,32,24,16,8,0},{121,113,105,97,89,8..., dimensions={0} | all-to-all | bytes 1048576 | tf_op jit(solution)/shard_map/all_to_all | solution.py:317
  54.3 0.8 %shard_map.85 = f32[32,2048]{1,0:T(8,128)} custom-call(bf16[16,8,16,128]{3,2,1,0:T(8,128)(2,1)S(1)} %all_to_all.11.arr), custom_call_target="tpu_custom_call" | custom-call | tf_op jit(solution)/shard_map/pallas_call | solution.py:320
Async XLA Ops:
  35.4 4.0 %collective-permute-start = (bf16[128,16,128]{2,1,0:T(8,128)(2,1)S(1)}, bf16[128,16,128]{2,1,0:T(8,128)(2,1)S(1)}, u32[]{:S(2)}, u32[]{:S(2)}) collective-permute-start(bf16[128,16,128]{2,1,0:T(8,128)(2,1)S(1)} %shard_map.84), channel_id=1, source_target_pairs={{0,1},{1,0},{2,3},{3,2},{4,5},{5,4},{6,7},{7,6},{8,9},{9,8},{10,11... | collective-permute-start | bytes 1572872 | tf_op jit(solution)/shard_map/ppermute | solution.py:314

commit v9 on v8

--- a/solution.py
+++ b/solution.py
@@ -242,7 +242,8 @@
             for side in range(2):
                 at = 2 * pair + side + 1
                 sides.append(main[at] + left[at] + right[at])
-            out[8 * (TILES - 1 - j // 2) + j % 2 * 4 + u] = jnp.concatenate(sides, 0).astype(out.dtype)
+            spot = TILES - 1 - j // 2 % 4 * 4 - j // 8
+            out[8 * spot + j % 2 * 4 + u] = jnp.concatenate(sides, 0).astype(out.dtype)
         return carry
 
     lax.fori_loop(0, SKY // 8, fill, 0, unroll=2)
@@ -251,7 +252,7 @@
 def gather(arr, out):
     for x in range(4):
         for u in range(8):
-            terms = [arr[TILES - 1 - 4 * y - x, u].astype(F32) for y in range(4)]
+            terms = [arr[TILES - 1 - 4 * x - y, u].astype(F32) for y in range(4)]
             total = (terms[0] + terms[1]) + (terms[2] + terms[3])
             for side in range(2):
                 at = (2 * u + side) * BLOCK
@@ -313,7 +314,10 @@
     sends, keeps = placed(True), placed(False)
     other = lax.ppermute(sends, "visit", [(i, i ^ 1) for i in range(8)])
     both = (keeps + other.astype(F32)).astype(BF16).reshape(TILES, 8, STRIP, BLOCK)
-    backward = [[8 * t + visit for t in reversed(range(TILES))] for visit in range(8)]
+    backward = [
+        [8 * (4 * y + x) + visit for x in reversed(range(4)) for y in reversed(range(4))]
+        for visit in range(8)
+    ]
     parts = lax.all_to_all(
         both, ("tile", "visit"), split_axis=0, concat_axis=0, tiled=True, axis_index_groups=backward
     )

time: 55.3 us -> 55.9 us (1.011)
  no operation moved by 1% of the time
where the time goes in v9:
time: 55.9 us; the launch traced here: 55.7 us
  blocking collectives  39.5 us (71%)
  Pallas kernels  14.1 us (25%)
  starting transfers between devices  1.9 us (3%)
    all_to_all x1, blocking collectives, on_device(): lax.all_to_all(sent, ('tile', 'visit'), split_axis=0, concat_axis=0, tile...  24.6 us
    all_to_all x1, blocking collectives, on_device(): lax.all_to_all(both, ('tile', 'visit'), split_axis=0, concat_axis=0, tile...  15 us
    pallas_call x1, Pallas kernels, on_device(): pl.pallas_call(contribute, out_shape=jax.ShapeDtypeStruct((TILES, STRIP,...  8.71 us
    pallas_call x2, Pallas kernels, placed(): pl.pallas_call(functools.partial(place, goes), out_shape=jax.ShapeDtypeSt...  4.6 us
    ppermute x1, starting transfers between devices, on_device(): other = lax.ppermute(sends, 'visit', [(i, i ^ 1) for i in range(8)])  1.9 us
  transfers between devices with their start and end apart: 1, of which 0 were waited for; matrix products, arithmetic and copies ran while one was open for 0% of the time, Pallas kernels for 4%

profile of v9, /device:TPU:1, one launch (start us, length us, event | category | flops | bytes accessed | tf_op | source)
XLA Modules:
  0.0 55.7 jit_solution(10064850743555360060)
XLA Ops:
  0.0 8.7 %shard_map.82 = bf16[16,16,2304]{2,1,0:T(8,128)(2,1)} custom-call(s32[2,14]{1,0:T(2,128)} %bitcast.5, s32[1,14]{1,0:T(1,128)} %dest_in.1, f32[1,9]{1,0:T(1,128)} %coef_in.1, f32[8]{0:T(128)} %vw_in.1, f32[32,384]{1,0:T(8,128)} %constant.2.clone.tab_in, bf16[9,31]{1,0:T(8,128)(2,1)} %brow_in.1, bf16[9,31]{1,0:T(8,128)(2,1)} %bcol_in.1, ...), custom_call_target="tpu_custom_call" | custom-call | tf_op jit(solution)/shard_map/pallas_call | solution.py:264
  8.7 24.6 %all_to_all.10.arr = bf16[16,16,2304]{2,1,0:T(8,128)(2,1)S(1)} all-to-all(bf16[16,16,2304]{2,1,0:T(8,128)(2,1)} %shard_map.82), channel_id=1, replica_groups={{30,22,14,6,28,20,12,4,26,18,10,2,24,16,8,0},{62,54,46,38,60,52,44,36,5..., dimensions={0} | all-to-all | bytes 2359296 | tf_op jit(solution)/shard_map/all_to_all | solution.py:294
  33.3 2.3 %shard_map.84 = bf16[128,16,128]{2,1,0:T(8,128)(2,1)S(1)} custom-call(bf16[16,16,2304]{2,1,0:T(8,128)(2,1)S(1)} %all_to_all.10.arr), custom_call_target="tpu_custom_call" | custom-call | flops 10000000 | bytes 4000000 | tf_op jit(solution)/shard_map/pallas_call | solution.py:299
  35.6 1.9 %collective-permute-start = (bf16[128,16,128]{2,1,0:T(8,128)(2,1)S(1)}, bf16[128,16,128]{2,1,0:T(8,128)(2,1)S(1)}, u32[]{:S(2)}, u32[]{:S(2)}) collective-permute-start(bf16[128,16,128]{2,1,0:T(8,128)(2,1)S(1)} %shard_map.84), channel_id=1, source_target_pairs={{0,1},{1,0},{2,3},{3,2},{4,5},{5,4},{6,7},{7,6},{8,9},{9,8},{10,11... | collective-permute-start | bytes 1572872 | tf_op jit(solution)/shard_map/ppermute | solution.py:315
  37.5 2.3 %shard_map.83 = f32[128,16,128]{2,1,0:T(8,128)S(1)} custom-call(bf16[16,16,2304]{2,1,0:T(8,128)(2,1)S(1)} %all_to_all.10.arr), custom_call_target="tpu_custom_call" | custom-call | flops 10000000 | bytes 4000000 | tf_op jit(solution)/shard_map/pallas_call | solution.py:299
  39.8 0.0 collective-permute-done
  39.8 0.1 add_convert_fusion
  39.9 15.0 %all_to_all.11.arr = bf16[16,8,16,128]{3,2,1,0:T(8,128)(2,1)S(1)} all-to-all(bf16[16,8,16,128]{3,2,1,0:T(8,128)(2,1)S(1)} %bitcast.4), channel_id=1, replica_groups={{120,88,56,24,112,80,48,16,104,72,40,8,96,64,32,0},{121,89,57,25,113,81..., dimensions={0} | all-to-all | bytes 1048576 | tf_op jit(solution)/shard_map/all_to_all | solution.py:321
  54.9 0.8 %shard_map.85 = f32[32,2048]{1,0:T(8,128)} custom-call(bf16[16,8,16,128]{3,2,1,0:T(8,128)(2,1)S(1)} %all_to_all.11.arr), custom_call_target="tpu_custom_call" | custom-call | tf_op jit(solution)/shard_map/pallas_call | solution.py:324
Async XLA Ops:
  35.6 4.2 %collective-permute-start = (bf16[128,16,128]{2,1,0:T(8,128)(2,1)S(1)}, bf16[128,16,128]{2,1,0:T(8,128)(2,1)S(1)}, u32[]{:S(2)}, u32[]{:S(2)}) collective-permute-start(bf16[128,16,128]{2,1,0:T(8,128)(2,1)S(1)} %shard_map.84), channel_id=1, source_target_pairs={{0,1},{1,0},{2,3},{3,2},{4,5},{5,4},{6,7},{7,6},{8,9},{9,8},{10,11... | collective-permute-start | bytes 1572872 | tf_op jit(solution)/shard_map/ppermute | solution.py:315
